TPU v7x, 512 devices: a whole 4x4x16 slice. The times are simulated.
512 devices in a mesh: seq: 64 (over z, y), tp: 8 (over x, core).
Axes of the slice: x: 4, y: 4, z: 16, core: 2. Of those that a mesh axis runs over, the one named last changes fastest.
Arguments:
- queries: bfloat16 [64, 64, 128], P('seq', 'tp'), may hold values from -160 to 160
- key_codes: bfloat16 [524288, 8, 128], P('seq', 'tp'), may hold values from -127 to 127, as said below
- key_scale: float32 [4096, 8, 128], P('seq', 'tp'), may hold values from 0.005 to 0.03
- outlier_chan: int32 [4096, 8, 8], P('seq', 'tp'), may hold values from 0 to 127
- outlier_val: bfloat16 [524288, 8, 8], P('seq', 'tp'), may hold values from -12 to 12
- value_codes: bfloat16 [524288, 8, 128], P('seq', 'tp'), may hold values from -127 to 127, as said below
- value_scale: float32 [4096, 8, 128], P('seq', 'tp'), may hold values from 0.005 to 0.03
- suffix_keys: bfloat16 [256, 128, 8, 128], P('seq', None, 'tp'), may hold values from -10 to 10
- suffix_values: bfloat16 [256, 128, 8, 128], P('seq', None, 'tp'), may hold values from -6 to 6
- page_table: int32 [64, 4], P('seq'), may hold values from 0 to 3, as said below
- suffix_len: int32 [64], P('seq'), may hold values from 1 to 512, as said below
- out_weight: bfloat16 [8192, 8192], P('tp', 'seq'), may hold values from -0.5 to 0.5
Outputs:
- output: bfloat16 [64, 8192], P('tp', 'seq')
Inputs may be any that keep to these rules, and one draw needn't show every extreme that they name: `key_codes`: whole numbers. `value_codes`: whole numbers. `page_table`: the 1 samples b with the same b // 1 name each of the 4 pages of their pool exactly once. `suffix_len`: some sample has all 512 positions live.
All inputs are finite; a program needn't handle non-finite values.
Results may differ from a plain program's by a relative error of at most 0.018.
The roundings to bfloat16 on the way count: a program that leaves them out, or rounds other values in their place, can miss the bound.
Values may be sent and summed in bfloat16 or wider, within the bound.
No kernel may reach another device: no remote copies, remote signals or barrier semaphores. Data moves between devices by JAX's collectives and lax.ppermute only.
A program may use at most 64 MiB of HBM per device.

v0:
```python
import math

import jax
import jax.numpy as jnp
from jax import lax
from jax.sharding import PartitionSpec as P


def merged_2(part, axis, combine):
    gathered = jax.tree.map(lambda a: lax.all_gather(a, axis), part)

    def take(source):
        return jax.tree.map(lambda a: lax.dynamic_index_in_dim(a, source, 0, False), gathered)

    return lax.fori_loop(
        1, lax.axis_size(axis), lambda source, state: combine(state, take(source)), take(0)
    )


def restore(code_block, scale_block, channels, corrections):
    page_count = scale_block.shape[0]
    key_rows = code_block.shape[0]
    groups = code_block.shape[1]
    head_size = code_block.shape[2]
    page_rows = key_rows // page_count
    slots = channels.shape[2]
    onehot = (
        channels[..., None]
        == lax.broadcasted_iota(jnp.int32, (page_count, groups, slots, head_size), 3)
    ).astype(jnp.bfloat16)
    correction = jnp.einsum(
        "ptgo,pgoc->ptgc",
        corrections.reshape(page_count, page_rows, groups, slots),
        onehot,
        preferred_element_type=jnp.float32,
    )
    base = (
        code_block.reshape(page_count, page_rows, groups, head_size).astype(jnp.float32)
        * scale_block[:, None]
    )
    return (base + correction).reshape(key_rows, groups, head_size).astype(jnp.bfloat16)


def restore_plain(code_block, scale_block):
    page_count = scale_block.shape[0]
    key_rows = code_block.shape[0]
    groups = code_block.shape[1]
    head_size = code_block.shape[2]
    base = (
        code_block.reshape(page_count, key_rows // page_count, groups, head_size).astype(
            jnp.float32
        )
        * scale_block[:, None]
    )
    return base.reshape(key_rows, groups, head_size).astype(jnp.bfloat16)


def fold_parts(first, second):
    peak_one, total_one, weighted_one = first
    peak_two, total_two, weighted_two = second
    new_peak = jnp.maximum(peak_one, peak_two)
    fade_one = jnp.exp(peak_one - new_peak)
    fade_two = jnp.exp(peak_two - new_peak)
    return (
        new_peak,
        total_one * fade_one + total_two * fade_two,
        weighted_one * fade_one[..., None] + weighted_two * fade_two[..., None],
    )


def shards(
    queries,
    key_codes,
    key_scale,
    outlier_chan,
    outlier_val,
    value_codes,
    value_scale,
    suffix_keys,
    suffix_values,
    page_table,
    suffix_len,
    out_weight,
):
    local_count = queries.shape[0]
    heads = queries.shape[1]
    head_size = queries.shape[2]
    groups = key_codes.shape[1]
    per_group = heads // groups
    score_scale = 1.0 / math.sqrt(head_size)
    all_queries = lax.all_gather(queries, "seq", axis=0, tiled=True)
    sample_count = all_queries.shape[0]
    query_groups = all_queries.reshape(sample_count, groups, per_group, head_size)
    key_count = key_codes.shape[0]
    page_rows = key_count // key_scale.shape[0]
    block_rows = math.gcd(key_count, 512)
    block_pages = block_rows // page_rows

    def advance(running, block_index):
        peak_in, total_in, weighted_in = running
        first_key = block_index * block_rows
        first_page = block_index * block_pages
        key_block = restore(
            lax.dynamic_slice_in_dim(key_codes, first_key, block_rows, 0),
            lax.dynamic_slice_in_dim(key_scale, first_page, block_pages, 0),
            lax.dynamic_slice_in_dim(outlier_chan, first_page, block_pages, 0),
            lax.dynamic_slice_in_dim(outlier_val, first_key, block_rows, 0),
        )
        value_block = restore_plain(
            lax.dynamic_slice_in_dim(value_codes, first_key, block_rows, 0),
            lax.dynamic_slice_in_dim(value_scale, first_page, block_pages, 0),
        )
        scores = (
            jnp.einsum(
                "bgqc,tgc->bgqt", query_groups, key_block, preferred_element_type=jnp.float32
            )
            * score_scale
        )
        new_peak = jnp.maximum(peak_in, jnp.max(scores, axis=-1))
        rescale = jnp.exp(peak_in - new_peak)
        weights = jnp.exp(scores - new_peak[..., None])
        total_out = total_in * rescale + jnp.sum(weights, axis=-1)
        weighted_out = weighted_in * rescale[..., None] + jnp.einsum(
            "bgqt,tgc->bgqc",
            weights.astype(jnp.bfloat16),
            value_block,
            preferred_element_type=jnp.float32,
        )
        return ((new_peak, total_out, weighted_out), None)

    state_shape = (sample_count, groups, per_group)
    start_state = (
        jnp.full(state_shape, -1e30, jnp.float32),
        jnp.zeros(state_shape, jnp.float32),
        jnp.zeros(state_shape + (head_size,), jnp.float32),
    )
    (prefix_peak, prefix_total, prefix_weighted), ignored = lax.scan(
        advance, start_state, jnp.arange(key_count // block_rows, dtype=jnp.int32)
    )
    prefix_peak = prefix_peak.reshape(sample_count, heads)
    prefix_total = prefix_total.reshape(sample_count, heads)
    prefix_weighted = prefix_weighted.reshape(sample_count, heads, head_size)
    sample_keys = suffix_keys[page_table].reshape(local_count, -1, groups, head_size)
    sample_values = suffix_values[page_table].reshape(local_count, -1, groups, head_size)
    span = sample_keys.shape[1]
    own_queries = queries.reshape(local_count, groups, per_group, head_size)
    suffix_scores = (
        jnp.einsum("bgqc,bsgc->bgqs", own_queries, sample_keys, preferred_element_type=jnp.float32)
        * score_scale
    )
    live = lax.broadcasted_iota(jnp.int32, (local_count, span), 1) < suffix_len[:, None]
    suffix_scores = jnp.where(live[:, None, None, :], suffix_scores, -1e30)
    suffix_peak = jnp.max(suffix_scores, axis=-1)
    suffix_weights = jnp.exp(suffix_scores - suffix_peak[..., None])
    suffix_total = jnp.sum(suffix_weights, axis=-1)
    suffix_weighted = jnp.einsum(
        "bgqs,bsgc->bgqc",
        suffix_weights.astype(jnp.bfloat16),
        sample_values,
        preferred_element_type=jnp.float32,
    )
    suffix_peak = suffix_peak.reshape(local_count, heads)
    suffix_total = suffix_total.reshape(local_count, heads)
    suffix_weighted = suffix_weighted.reshape(local_count, heads, head_size)
    first_sample = lax.axis_index("seq") * local_count
    merged = merged_2((prefix_peak, prefix_total, prefix_weighted), "seq", fold_parts)
    own_peak = lax.dynamic_slice_in_dim(merged[0], first_sample, local_count, 0)
    own_total = lax.dynamic_slice_in_dim(merged[1], first_sample, local_count, 0)
    own_weighted = lax.dynamic_slice_in_dim(merged[2], first_sample, local_count, 0)
    final_peak, final_total, final_weighted = fold_parts(
        (own_peak, own_total, own_weighted), (suffix_peak, suffix_total, suffix_weighted)
    )
    attention = (
        (final_weighted / final_total[..., None])
        .astype(jnp.bfloat16)
        .reshape(local_count, heads * head_size)
    )
    gathered = lax.all_gather(attention, "seq", axis=0, tiled=True)
    return lax.psum_scatter(
        jnp.dot(gathered, out_weight, preferred_element_type=jnp.float32).astype(jnp.bfloat16),
        "tp",
        scatter_dimension=0,
        tiled=True,
    )


def solution(mesh):
    return jax.shard_map(
        shards,
        mesh=mesh,
        in_specs=(
            P("seq", "tp", None),
            P("seq", "tp", None),
            P("seq", "tp", None),
            P("seq", "tp", None),
            P("seq", "tp", None),
            P("seq", "tp", None),
            P("seq", "tp", None),
            P("seq", None, "tp", None),
            P("seq", None, "tp", None),
            P("seq", None),
            P("seq"),
            P("tp", "seq"),
        ),
        out_specs=P("tp", "seq"),
        check_vma=False,
    )
```

profile of v0, /device:TPU:1, one launch (start us, length us, event | category | flops | bytes accessed | tf_op | source)
XLA Modules:
  0.0 636.6 jit_solution(15295273830549116465)
XLA Ops:
  6.5 81.2 %all_gather.15 = bf16[64,8,128]{2,1,0:T(8,128)(2,1)S(1)} all-gather(bf16[1,8,128]{2,1,0:T(8,128)(2,1)} %param.16), channel_id=1, replica_groups=mesh['seq'=64,'tp'=8] {'seq'}, dimensions={0}, use_global_device_ids=true | all-gather | bytes 133120 | tf_op jit(solution)/shard_map/all_gather | solution.py:91
  88.5 107.9 %while.35 = (s32[]{:T(128)}, f32[64,1,8]{0,2,1:T(8,128)S(1)}, f32[64,1,8]{0,2,1:T(8,128)S(1)}, f32[64,1,8,128]{3,0,2,1:T(8,128)S(1)}, s32[16]{0:T(128)S(1)}, /*i...) while((s32[]{:T(128)}, f32[64,1,8]{0,2,1:T(8,128)S(1)}, ...), condition=%wide.region_3.4_spmd.clone, body=%wide.region_0.3_spmd.clone.sunk | while | flops 137501696 | bytes 4903597 | solution.py:137
  197.3 77.7 %all-gather = f32[4096,1,8]{2,1,0:T(1,128)S(1)} all-gather(f32[64,1,8]{2,1,0:T(1,128)S(1)} %copy.44), channel_id=2, replica_groups=mesh['seq'=64,'tp'=8] {'seq'}, dimensions={0}, use_global_device_ids=true | all-gather | bytes 133120 | tf_op jit(solution)/shard_map/all_gather | solution.py:10
  275.7 84.6 %all-gather.1 = f32[4096,1,8]{2,1,0:T(1,128)S(1)} all-gather(f32[64,1,8]{2,1,0:T(1,128)S(1)} %copy.45), channel_id=3, replica_groups=mesh['seq'=64,'tp'=8] {'seq'}, dimensions={0}, use_global_device_ids=true | all-gather | bytes 133120 | tf_op jit(solution)/shard_map/all_gather | solution.py:10
  362.9 1.3 dynamic-slice
  365.2 58.5 %all-gather.6.cloned.1.call-done = f32[4096,1,8,128]{3,0,2,1:T(8,128)} async-done(((f32[64,1,8,128]{3,0,2,1:T(8,128)}), f32[4096,1,8,128]{3,0,2,1:T(8,128)}) %all-gather.6.cloned.1.call-update) | async-done | bytes 16777232 | tf_op jit(solution)/shard_map/all_gather | solution.py:10
  424.9 93.9 %while.34 = (s32[]{:T(128)}, f32[64,8]{0,1:T(8,128)S(1)}, f32[64,8]{0,1:T(8,128)S(1)}, f32[64,8,128]{2,1,0:T(8,128)S(1)}, f32[64,64,8]{1,2,0:T(8,128)S(1)}, /*in...) while((s32[]{:T(128)}, f32[64,8]{0,1:T(8,128)S(1)}, ...), condition=%wide.region_5.6_spmd, body=%wide.region_4.5_spmd.sunk | while | flops 199685 | bytes 1339543 | solution.py:15
  425.1 1.0 constant_dynamic-slice_fusion.7
  426.6 1.0 constant_dynamic-slice_fusion.7
  428.0 1.0 constant_dynamic-slice_fusion.7
  429.5 1.0 constant_dynamic-slice_fusion.7
  431.0 1.0 constant_dynamic-slice_fusion.7
  432.5 1.0 constant_dynamic-slice_fusion.7
  434.0 1.0 constant_dynamic-slice_fusion.7
  435.5 1.0 constant_dynamic-slice_fusion.7
  437.0 1.0 constant_dynamic-slice_fusion.7
  438.5 1.0 constant_dynamic-slice_fusion.7
  440.0 1.0 constant_dynamic-slice_fusion.7
  441.5 1.0 constant_dynamic-slice_fusion.7
  442.9 1.0 constant_dynamic-slice_fusion.7
  444.4 1.0 constant_dynamic-slice_fusion.7
  445.9 1.0 constant_dynamic-slice_fusion.7
  519.1 61.6 %all-gather.3 = bf16[64,1,1024]{2,1,0:T(2,128)(2,1)S(1)} all-gather(bf16[1,1,1024]{2,1,0:T(2,128)(2,1)S(1)} %reshape.193), channel_id=1, replica_groups=mesh['seq'=64,'tp'=8] {'seq'}, dimensions={0}, use_global_device_ids=true | all-gather | bytes 133120 | tf_op jit(solution)/shard_map/all_gather | solution.py:178
  580.9 48.2 %all-reduce = bf16[64,128]{1,0:T(8,128)(2,1)S(1)} all-reduce(bf16[64,128]{1,0:T(8,128)(2,1)S(1)} %convolution_convert_fusion), channel_id=5, replica_groups=mesh['seq'=64,'tp'=8] {'tp'}, use_global_device_ids=true, to_apply=%region_8.9.clone | all-reduce | flops 8192 | bytes 32768
  (536 shorter events, 170.2 us)
Async XLA Ops:
  6.5 574.2 %copy-start = (bf16[1024,128]{1,0:T(8,128)(2,1)S(1)}, bf16[1024,128]{1,0:T(8,128)(2,1)}, u32[]{:S(2)}) copy-start(bf16[1024,128]{1,0:T(8,128)(2,1)} %param.27) | copy-start | bytes 786436
  6.5 417.2 %all-gather.6.cloned.1.call-start = ((), (), s32[]{:S(2)}) async-start(), calls=%async_computation | async-start | bytes 17039360 | tf_op jit(solution)/shard_map/all_gather | solution.py:10
  196.5 0.7 copy-start.1
  275.6 86.0 %copy-start.5 = (s32[1,4]{1,0:T(1,128)S(1)}, s32[1,4]{1,0:T(1,128)}, u32[]{:S(2)}) copy-start(s32[1,4]{1,0:T(1,128)} %param.25) | copy-start | bytes 52
  275.6 86.0 %copy-start.2 = (bf16[4,128,1,128]{3,1,2,0:T(8,128)(2,1)S(1)}, bf16[4,128,1,128]{3,1,2,0:T(8,128)(2,1)}, u32[]{:S(2)}) copy-start(bf16[4,128,1,128]{3,1,2,0:T(8,128)(2,1)} %param.23) | copy-start | bytes 393220
  275.6 86.6 %copy-start.3 = (bf16[4,128,1,128]{3,1,2,0:T(8,128)(2,1)S(1)}, bf16[4,128,1,128]{3,1,2,0:T(8,128)(2,1)}, u32[]{:S(2)}) copy-start(bf16[4,128,1,128]{3,1,2,0:T(8,128)(2,1)} %param.24) | copy-start | bytes 393220
  275.7 89.1 %copy-start.4 = (bf16[1,8,128]{2,1,0:T(8,128)(2,1)S(1)}, bf16[1,8,128]{2,1,0:T(8,128)(2,1)}, u32[]{:S(2)}) copy-start(bf16[1,8,128]{2,1,0:T(8,128)(2,1)} %param.16) | copy-start | bytes 6148
Sparse Core Ops, SparseCore 0:
  197.3 226.3 all-gather.5
where the time goes:
time: 641 us; the launch traced here: 637 us
  blocking collectives  353 us (55%)
  local copies, waits for them, and re-layouts  116 us (18%)
  waiting for transfers between devices  58.5 us (9%)
  other arithmetic  41.4 us (6%)
  matrix products  28.8 us (4%)
  loops' own time  24 us (4%)
  between operations  14.8 us (2%)
    all_gather x2, blocking collectives, merged_2(): gathered = jax.tree.map(lambda a: lax.all_gather(a, axis), part)  162 us
    all_gather x1, blocking collectives, shards(): all_queries = lax.all_gather(queries, 'seq', axis=0, tiled=True)  81.2 us
    all_gather x1, blocking collectives, shards(): gathered = lax.all_gather(attention, 'seq', axis=0, tiled=True)  61.6 us
    dynamic_slice x65, local copies, waits for them, and re-layouts, take(): lax.dynamic_index_in_dim(a, source, 0, False)  61.1 us
    all_gather x1, waiting for transfers between devices, merged_2(): gathered = jax.tree.map(lambda a: lax.all_gather(a, axis), part)  58.5 us
    unnamed x1, blocking collectives  48.2 us
    another operation x1, loops' own time, shards(): lax.scan(advance, start_state, jnp.arange(key_count // block_rows, dtype=...  21.8 us
    add x63, other arithmetic, fold_parts(): weighted_one * fade_one[..., None] + weighted_two * fade_two[..., None]  19 us
  transfers between devices with their start and end apart: 1, of which 1 were waited for; matrix products, arithmetic and copies ran while one was open for 1% of the time, Pallas kernels for 0%

commit v1 on v0

v1 whole, which is shorter than its diff:
```python
import functools
import math

import jax
import jax.numpy as jnp
from jax import lax
from jax.experimental import pallas as pl
from jax.experimental.pallas import tpu as pltpu
from jax.sharding import Mesh, PartitionSpec as P

F32 = jnp.float32
BF16 = jnp.bfloat16
LANES = 128
HEADS = 8
PAGE = 128
TILE = 256
BLOCK = 1024
SPLIT = 32
STATS = 16
LOW = -1e30
VMEM = pl.BlockSpec(memory_space=pltpu.VMEM)
SMEM = pl.BlockSpec(memory_space=pltpu.SMEM)
ANY = pl.BlockSpec(memory_space=pl.ANY)
LIMIT = 48 * 1024 * 1024


def nt(a, b):
    return lax.dot_general(a, b, (((1,), (1,)), ((), ())), preferred_element_type=F32)


def split_rows(row):
    high = row.astype(BF16).astype(F32)
    rest = row - high
    middle = rest.astype(BF16).astype(F32)
    low = rest - middle
    part = lax.broadcasted_iota(jnp.int32, row.shape, row.ndim - 1) // SPLIT
    kept = jnp.where(part == 0, high, jnp.where(part == 1, middle, low))
    return jnp.where(part < 3, kept, 0.0).astype(BF16)


def to_lanes(columns):
    row = lax.broadcasted_iota(jnp.int32, columns.shape, 0)
    lane = lax.broadcasted_iota(jnp.int32, columns.shape, 1)
    return jnp.sum(jnp.where(lane % SPLIT == row, columns, 0.0), axis=0, keepdims=True)


def to_rows(stat):
    wide = jnp.broadcast_to(stat, (SPLIT, LANES))
    row = lax.broadcasted_iota(jnp.int32, wide.shape, 0)
    lane = lax.broadcasted_iota(jnp.int32, wide.shape, 1)
    return jnp.sum(jnp.where(lane % SPLIT == row, wide, 0.0), axis=1, keepdims=True)


def attend_kernel(
    own_ref,
    len_ref,
    table_ref,
    q_ref,
    own_q_ref,
    kscale_ref,
    chan_ref,
    outlier_ref,
    vscale_ref,
    kcodes_hbm,
    vcodes_hbm,
    skeys_hbm,
    svalues_hbm,
    out_ref,
    kbuf,
    vbuf,
    skbuf,
    svbuf,
    scores,
    peak,
    total,
    acc,
    ksem,
    vsem,
    ssem,
):
    keys = kbuf.shape[0]
    blocks = keys // BLOCK
    queries = q_ref.shape[0]
    score_scale = math.log2(math.e) / math.sqrt(LANES)

    def chunk(hbm, buf, sem, i):
        rows = pl.ds(pl.multiple_of(i * BLOCK, BLOCK), BLOCK)
        return pltpu.make_async_copy(hbm.at[rows, :], buf.at[rows, :], sem.at[i])

    for i in range(blocks):
        chunk(kcodes_hbm, kbuf, ksem, i).start()
    skeys = pltpu.make_async_copy(skeys_hbm, skbuf, ssem.at[0])
    svalues = pltpu.make_async_copy(svalues_hbm, svbuf, ssem.at[1])
    skeys.start()
    svalues.start()
    for i in range(blocks):
        chunk(vcodes_hbm, vbuf, vsem, i).start()

    peak[...] = jnp.full(peak.shape, LOW, F32)
    page_lane = lax.broadcasted_iota(jnp.int32, chan_ref.shape, 1)
    channel = lax.broadcasted_iota(jnp.int32, (HEADS, LANES), 1)

    @pl.loop(0, blocks)
    def score_block(i):
        chunk(kcodes_hbm, kbuf, ksem, i).wait()
        running = peak[...]
        for j in range(BLOCK // TILE):
            parts = []
            for p in range(TILE // PAGE):
                page = i * (BLOCK // PAGE) + j * (TILE // PAGE) + p
                rows = pl.ds(pl.multiple_of(page * PAGE, PAGE), PAGE)
                chosen = jnp.sum(
                    jnp.where(page_lane == page, chan_ref[...], 0), axis=1, keepdims=True
                )
                onehot = (channel == chosen).astype(BF16)
                correction = lax.dot_general(
                    outlier_ref[:, rows],
                    onehot,
                    (((0,), (0,)), ((), ())),
                    preferred_element_type=F32,
                )
                parts.append((kbuf[rows, :].astype(F32) * kscale_ref[page] + correction).astype(BF16))
            tile = nt(q_ref[...], jnp.concatenate(parts, axis=0))
            scores[i * (BLOCK // TILE) + j] = tile
            running = jnp.maximum(running, jnp.maximum(tile[:, :LANES], tile[:, LANES:]))
        peak[...] = running

    peak[...] = jnp.broadcast_to(
        jnp.max(peak[...], axis=1, keepdims=True) * score_scale, peak.shape
    )
    total[...] = jnp.zeros(total.shape, F32)
    acc[...] = jnp.zeros(acc.shape, F32)

    @pl.loop(0, blocks)
    def value_block(i):
        chunk(vcodes_hbm, vbuf, vsem, i).wait()
        running = total[...]
        top = peak[...]
        weights, values = [], []
        for j in range(BLOCK // TILE):
            for p in range(TILE // PAGE):
                page = i * (BLOCK // PAGE) + j * (TILE // PAGE) + p
                rows = pl.ds(pl.multiple_of(page * PAGE, PAGE), PAGE)
                values.append((vbuf[rows, :].astype(F32) * vscale_ref[page]).astype(BF16))
                part = scores[i * (BLOCK // TILE) + j, :, p * LANES : (p + 1) * LANES]
                weight = jnp.exp2(part * score_scale - top)
                running = running + weight
                weights.append(weight.astype(BF16))
        total[...] = running
        acc[...] += jnp.dot(
            jnp.concatenate(weights, axis=1),
            jnp.concatenate(values, axis=0),
            preferred_element_type=F32,
        )

    total[...] = jnp.broadcast_to(jnp.sum(total[...], axis=1, keepdims=True), total.shape)

    skeys.wait()
    svalues.wait()
    own = pl.ds(pl.multiple_of(own_ref[0] * HEADS, HEADS), HEADS)
    live = len_ref[0]
    place = lax.broadcasted_iota(jnp.int32, (HEADS, PAGE), 1)
    own_scores = [
        jnp.where(
            place + j * PAGE < live,
            nt(own_q_ref[...], skbuf[table_ref[0, j]]) * score_scale,
            LOW,
        )
        for j in range(skbuf.shape[0])
    ]
    top = peak[own, :]
    for part in own_scores:
        top = jnp.maximum(top, jnp.max(part, axis=1, keepdims=True))
    fade = jnp.exp2(peak[own, :] - top)
    sums = total[own, :] * fade
    weighted = acc[own, :] * fade
    for j, part in enumerate(own_scores):
        weight = jnp.where(place + j * PAGE < live, jnp.exp2(part - top), 0.0)
        sums = sums + jnp.sum(weight, axis=1, keepdims=True)
        weighted = weighted + jnp.dot(
            weight.astype(BF16), svbuf[table_ref[0, j]], preferred_element_type=F32
        )
    peak[own, :] = top
    total[own, :] = sums
    acc[own, :] = weighted

    for z in range(queries // SPLIT):
        rows = slice(z * SPLIT, (z + 1) * SPLIT)
        out_ref[z, :SPLIT, :] = (acc[rows, :] / total[rows, :]).astype(BF16)
        stat = split_rows(to_lanes(peak[rows, :] + jnp.log2(total[rows, :])))
        out_ref[z, SPLIT:, :] = jnp.broadcast_to(stat, (STATS, LANES))


def merge_kernel(in_ref, out_ref):
    sources = in_ref.shape[0]
    logs = [to_rows(in_ref[s, SPLIT:, :].astype(F32)[:1]) for s in range(sources)]
    top = functools.reduce(jnp.maximum, logs)
    sums = jnp.zeros(top.shape, F32)
    weighted = jnp.zeros((SPLIT, LANES), F32)
    for s in range(sources):
        weight = jnp.exp2(logs[s] - top)
        sums = sums + weight
        weighted = weighted + in_ref[s, :SPLIT, :].astype(F32) * weight
    merged = (weighted / sums).astype(BF16)
    copies, rows, lanes = out_ref.shape
    if rows > SPLIT:
        wide = jnp.broadcast_to(top + jnp.log2(sums), (SPLIT, LANES))
        stat = jnp.broadcast_to(split_rows(to_lanes(wide)), (STATS, LANES))
    for c in range(copies):
        out_ref[c, :SPLIT, :] = merged
        if rows > SPLIT:
            out_ref[c, SPLIT:, :] = stat


def project_kernel(in_ref, weight_ref, out_ref, wide):
    blocks = in_ref.shape[0]
    for z in range(blocks):
        wide[z * SPLIT : (z + 1) * SPLIT, :] = in_ref[z].astype(F32)
    samples = blocks * SPLIT // HEADS
    result = jnp.zeros((samples, LANES), F32)
    for h in range(HEADS):
        part = wide[pl.ds(h, samples, stride=HEADS), :].astype(BF16)
        result = result + jnp.dot(
            part, weight_ref[h * LANES : (h + 1) * LANES, :], preferred_element_type=F32
        )
    out_ref[...] = result.astype(BF16)


def sum_kernel(in_ref, out_ref):
    result = in_ref[0].astype(F32)
    for c in range(1, in_ref.shape[0]):
        result = result + in_ref[c].astype(F32)
    out_ref[...] = result.astype(BF16)


def spread(block, axis):
    copies = jnp.broadcast_to(block[None], (lax.axis_size(axis),) + block.shape)
    return lax.all_to_all(copies, axis, 0, 0)


def attend(
    own,
    all_queries,
    queries,
    key_codes,
    key_scale,
    outlier_chan,
    outlier_val,
    value_codes,
    value_scale,
    suffix_keys,
    suffix_values,
    page_table,
    suffix_len,
    depth,
):
    rows = all_queries.shape[0]
    keys = key_codes.shape[0]
    pools = suffix_keys.shape[0]
    params = pltpu.CompilerParams(vmem_limit_bytes=LIMIT)
    return pl.pallas_call(
        attend_kernel,
        out_shape=jax.ShapeDtypeStruct((depth, SPLIT + STATS, LANES), BF16),
        in_specs=[SMEM] * 3 + [VMEM] * 6 + [ANY] * 4,
        out_specs=VMEM,
        scratch_shapes=[
            pltpu.VMEM((keys, LANES), BF16),
            pltpu.VMEM((keys, LANES), BF16),
            pltpu.VMEM((pools, PAGE, LANES), BF16),
            pltpu.VMEM((pools, PAGE, LANES), BF16),
            pltpu.VMEM((keys // TILE, rows, TILE), F32),
            pltpu.VMEM((rows, LANES), F32),
            pltpu.VMEM((rows, LANES), F32),
            pltpu.VMEM((rows, LANES), F32),
            pltpu.SemaphoreType.DMA((keys // BLOCK,)),
            pltpu.SemaphoreType.DMA((keys // BLOCK,)),
            pltpu.SemaphoreType.DMA((2,)),
        ],
        compiler_params=params,
        name="attend",
    )(
        own,
        suffix_len,
        page_table,
        all_queries,
        queries,
        key_scale,
        outlier_chan.reshape(-1, HEADS).T,
        outlier_val.reshape(-1, HEADS).T,
        value_scale,
        key_codes.reshape(keys, LANES),
        value_codes.reshape(keys, LANES),
        suffix_keys.reshape(pools, PAGE, LANES),
        suffix_values.reshape(pools, PAGE, LANES),
    )


def shards(
    queries,
    key_codes,
    key_scale,
    outlier_chan,
    outlier_val,
    value_codes,
    value_scale,
    suffix_keys,
    suffix_values,
    page_table,
    suffix_len,
    out_weight,
):
    depth, width = lax.axis_size("z"), lax.axis_size("y")
    samples = depth * width
    queries = queries.reshape(HEADS, LANES)
    all_queries = spread(spread(queries, "y"), "z").reshape(samples * HEADS, LANES)
    own = (lax.axis_index("z") * width + lax.axis_index("y")).astype(jnp.int32).reshape(1)
    params = pltpu.CompilerParams(vmem_limit_bytes=LIMIT)
    partial = attend(
        own,
        all_queries,
        queries,
        key_codes,
        key_scale,
        outlier_chan,
        outlier_val,
        value_codes,
        value_scale,
        suffix_keys,
        suffix_values,
        page_table,
        suffix_len,
        depth,
    )
    partial = lax.all_to_all(partial, "z", 0, 0)
    partial = pl.pallas_call(
        merge_kernel,
        out_shape=jax.ShapeDtypeStruct((width, SPLIT + STATS, LANES), BF16),
        in_specs=[VMEM],
        out_specs=VMEM,
        compiler_params=params,
        name="merge_z",
    )(partial)
    partial = lax.all_to_all(partial, "y", 0, 0)
    attention = pl.pallas_call(
        merge_kernel,
        out_shape=jax.ShapeDtypeStruct((depth, SPLIT, LANES), BF16),
        in_specs=[VMEM],
        out_specs=VMEM,
        compiler_params=params,
        name="merge_y",
    )(partial)
    attention = lax.all_to_all(attention, "z", 0, 0)
    product = pl.pallas_call(
        project_kernel,
        out_shape=jax.ShapeDtypeStruct((samples, LANES), BF16),
        in_specs=[VMEM, VMEM],
        out_specs=VMEM,
        scratch_shapes=[pltpu.VMEM((samples * HEADS, LANES), F32)],
        compiler_params=params,
        name="project",
    )(attention, out_weight)
    tp = lax.axis_size("x") * lax.axis_size("core")
    product = lax.all_to_all(product.reshape(tp, samples // tp, LANES), ("x", "core"), 0, 0)
    return pl.pallas_call(
        sum_kernel,
        out_shape=jax.ShapeDtypeStruct((samples // tp, LANES), BF16),
        in_specs=[VMEM],
        out_specs=VMEM,
        compiler_params=params,
        name="sum_tp",
    )(product)


def solution(mesh):
    grid = Mesh(mesh.devices.reshape(16, 4, 4, 2), ("z", "y", "x", "core"))
    seq, tp = ("z", "y"), ("x", "core")
    return jax.shard_map(
        shards,
        mesh=grid,
        in_specs=(
            P(seq, tp, None),
            P(seq, tp, None),
            P(seq, tp, None),
            P(seq, tp, None),
            P(seq, tp, None),
            P(seq, tp, None),
            P(seq, tp, None),
            P(seq, None, tp, None),
            P(seq, None, tp, None),
            P(seq, None),
            P(seq),
            P(tp, seq),
        ),
        out_specs=P(tp, seq),
        check_vma=False,
    )
```

time: 641 us -> 118 us (0.18)
  blocking collectives: 353 us -> 65.8 us
  local copies, waits for them, and re-layouts: 116 us -> 10.8 us
  waiting for transfers between devices: 58.5 us -> 11.4 us
  other arithmetic: 41.4 us -> 0 us
  matrix products: 28.8 us -> 0 us
  loops' own time: 24 us -> 0 us
  starting transfers between devices: 0.01 us -> 14.9 us
  between operations: 14.8 us -> 0.7 us
  Pallas kernels: 0 us -> 14.1 us
    all_gather x4 -> x0, blocking collectives: 305 us -> none  [the longest x2 162 us: merged_2(): gathered = jax.tree.map(lambda a: lax.all_gather(a, axis), part)]
    dynamic_slice x97 -> x0, local copies, waits for them, and re-layouts: 86.1 us -> none  [the longest x65 61.1 us: take(): lax.dynamic_index_in_dim(a, source, 0, False)]
    all_to_all x0 -> x5, blocking collectives: none -> 65.8 us  [the longest x1 18.6 us: shards(): attention = lax.all_to_all(attention, 'z', 0, 0)]
    all_gather x1 -> x0, waiting for transfers between devices: 58.5 us -> none  [merged_2(): gathered = jax.tree.map(lambda a: lax.all_gather(a, axis), part)]
    unnamed x1 -> x0, blocking collectives: 48.2 us -> none
    dot_general x51 -> x0, matrix products: 28.8 us -> none  [the longest x16 15.3 us: restore(): jnp.einsum('ptgo,pgoc->ptgc', corrections.reshape(page_count, page_rows,...]
    another operation x2 -> x0, loops' own time: 24 us -> none  [the longest x1 21.8 us: shards(): lax.scan(advance, start_state, jnp.arange(key_count // block_rows, dtype=...]
    add x142 -> x0, other arithmetic: 20.2 us -> none  [the longest x63 19 us: fold_parts(): weighted_one * fade_one[..., None] + weighted_two * fade_two[..., None]]
  transfers between devices with their start and end apart: 1 -> 1, of which waited for: 1 -> 1; matrix products, arithmetic and copies ran while one was open for 1% -> 0% of each run, Pallas kernels for 0% -> 0%
where the time goes in v1:
time: 118 us
  blocking collectives  65.8 us (56%)
  starting transfers between devices  14.9 us (13%)
  Pallas kernels  14.1 us (12%)
  waiting for transfers between devices  11.4 us (10%)
  local copies, waits for them, and re-layouts  10.8 us (9%)
    all_to_all x1, blocking collectives, shards(): attention = lax.all_to_all(attention, 'z', 0, 0)  18.6 us
    all_to_all x1, blocking collectives, shards(): partial = lax.all_to_all(partial, 'z', 0, 0)  16.1 us
    all_to_all x1, starting transfers between devices, spread(): return lax.all_to_all(copies, axis, 0, 0)  14.9 us
    all_to_all x1, blocking collectives, shards(): lax.all_to_all(product.reshape(tp, samples // tp, LANES), ('x', 'core'),...  14.5 us
    pallas_call x1, Pallas kernels, attend(): pl.pallas_call(attend_kernel, out_shape=jax.ShapeDtypeStruct((depth, SPLI...  12.9 us
    all_to_all x1, waiting for transfers between devices, spread(): return lax.all_to_all(copies, axis, 0, 0)  11.4 us
    unnamed x22, local copies, waits for them, and re-layouts  9.43 us
    all_to_all x1, blocking collectives, spread(): return lax.all_to_all(copies, axis, 0, 0)  8.97 us
  transfers between devices with their start and end apart: 1, of which 1 were waited for; matrix products, arithmetic and copies ran while one was open for 0% of the time, Pallas kernels for 0%

profile of v1, /device:TPU:1, one launch (start us, length us, event | category | flops | bytes accessed | tf_op | source)
XLA Modules:
  0.0 117.6 jit_solution(7611383524605675114)
XLA Ops:
  0.0 0.7 broadcast_in_dim.14
  0.7 9.0 %all_to_all.30 = bf16[4,8,128]{2,1,0:T(8,128)(2,1)S(1)} all-to-all(bf16[4,8,128]{2,1,0:T(8,128)(2,1)S(1)} %broadcast_in_dim.14), channel_id=1, replica_groups=mesh['z'=16,'y'=4,'x'=4,'core'=2] {'y'}, dimensions={0} | all-to-all | bytes 16384 | tf_op jit(solution)/shard_map/all_to_all | solution.py:238
  9.7 0.7 broadcast_in_dim.15
  10.3 14.9 %all-to-all-start.1 = ((bf16[16,4,8,128]{3,2,1,0:T(8,128)(2,1)}), bf16[16,4,8,128]{3,2,1,0:T(8,128)(2,1)S(1)}, u32[]{:S(2)}, u32[]{:S(2)}) async-start(bf16[16,4,8,128]{3,2,1,0:T(8,128)(2,1)} %broadcast_in_dim.15), calls=%async_computation.1 | async-start | bytes 262144 | tf_op jit(solution)/shard_map/all_to_all | solution.py:238
  25.9 11.4 %all-to-all-done.1 = bf16[16,4,8,128]{3,2,1,0:T(8,128)(2,1)S(1)} async-done(((bf16[16,4,8,128]{3,2,1,0:T(8,128)(2,1)}), bf16[16,4,8,128]{3,2,1,0:T(8,128)(2,1)S(1)}, u32[]{:S(2)}, u32[]{:S(2)}) %all-to-all-start.1) | async-done | bytes 131104 | tf_op jit(solution)/shard_map/all_to_all | solution.py:238
  37.3 1.6 %copy-done = bf16[8192,1,128]{2,0,1:T(8,128)(2,1)S(1)} copy-done((bf16[8192,1,128]{2,0,1:T(8,128)(2,1)S(1)}, bf16[8192,1,128]{2,0,1:T(8,128)(2,1)}, u32[]{:S(2)}) %copy-start) | copy-done | bytes 2097176
  38.8 1.6 %copy-done.1 = bf16[8192,1,128]{2,0,1:T(8,128)(2,1)S(1)} copy-done((bf16[8192,1,128]{2,0,1:T(8,128)(2,1)S(1)}, bf16[8192,1,128]{2,0,1:T(8,128)(2,1)}, u32[]{:S(2)}) %copy-start.1) | copy-done | bytes 2097176
  40.4 0.9 copy-done.3
  41.3 0.9 copy-done.4
  42.2 0.9 copy-done.5
  43.2 0.8 copy-done.6
  43.9 0.8 copy-done.7
  44.7 0.7 copy-done.8
  45.4 0.7 copy-done.9
  46.0 0.7 copy-done.10
  46.7 12.9 %attend.1 = bf16[16,48,128]{2,1,0:T(8,128)(2,1)S(1)} custom-call(s32[1]{0:T(128)} %bitcast.own_ref, s32[1]{0:T(128)S(6)} %copy.13.len_ref, s32[1,4]{1,0:T(1,128)S(1)} %copy-done.10, bf16[512,128]{1,0:T(8,128)(2,1)S(1)} %bitcast.16, bf16[8,128]{1,0:T(8,128)(2,1)S(1)} %bitcast.22, f32[64,1,128]{2,1,0:T(1,128)S(1)} %copy-done.6, s32[8,64]{1,0:T(8,128)S(1)} %bitcast.23, ...), custom_call_target="tpu_custom_call" | custom-call | tf_op jit(solution)/shard_map/attend/pallas_call | solution.py:261
  59.6 16.1 %all_to_all.31.in_ref = bf16[16,48,128]{2,1,0:T(8,128)(2,1)S(1)} all-to-all(bf16[16,48,128]{2,1,0:T(8,128)(2,1)S(1)} %attend.1), channel_id=1, replica_groups=mesh['z'=16,'y'=4,'x'=4,'core'=2] {'z'}, dimensions={0} | all-to-all | bytes 393216 | tf_op jit(solution)/shard_map/all_to_all | solution.py:334
  75.8 0.2 merge_z.1
  76.0 7.6 %all_to_all.32.in_ref = bf16[4,48,128]{2,1,0:T(8,128)(2,1)S(1)} all-to-all(bf16[4,48,128]{2,1,0:T(8,128)(2,1)S(1)} %merge_z.1), channel_id=1, replica_groups=mesh['z'=16,'y'=4,'x'=4,'core'=2] {'y'}, dimensions={0} | all-to-all | bytes 98304 | tf_op jit(solution)/shard_map/all_to_all | solution.py:343
  83.6 0.1 merge_y.1
  83.7 18.6 %all_to_all.33.in_ref = bf16[16,32,128]{2,1,0:T(8,128)(2,1)S(1)} all-to-all(bf16[16,32,128]{2,1,0:T(8,128)(2,1)S(1)} %merge_y.1), channel_id=1, replica_groups=mesh['z'=16,'y'=4,'x'=4,'core'=2] {'z'}, dimensions={0} | all-to-all | bytes 262144 | tf_op jit(solution)/shard_map/all_to_all | solution.py:352
  102.4 0.2 project.1
  102.5 14.5 %all_to_all.34.in_ref = bf16[8,8,128]{2,1,0:T(8,128)(2,1)S(1)} all-to-all(bf16[8,8,128]{2,1,0:T(8,128)(2,1)S(1)} %bitcast.20), channel_id=1, replica_groups=mesh['z'=16,'y'=4,'x'=4,'core'=2] {'x','core'}, dimensions={0} | all-to-all | bytes 32768 | tf_op jit(solution)/shard_map/all_to_all | solution.py:363
  117.0 0.6 sum_tp.1
  (12 shorter events, 0.0 us)
Async XLA Ops:
  10.3 26.9 %all-to-all-start.1 = ((bf16[16,4,8,128]{3,2,1,0:T(8,128)(2,1)}), bf16[16,4,8,128]{3,2,1,0:T(8,128)(2,1)S(1)}, u32[]{:S(2)}, u32[]{:S(2)}) async-start(bf16[16,4,8,128]{3,2,1,0:T(8,128)(2,1)} %broadcast_in_dim.15), calls=%async_computation.1 | async-start | bytes 262144 | tf_op jit(solution)/shard_map/all_to_all | solution.py:238
  37.3 1.6 %copy-start = (bf16[8192,1,128]{2,0,1:T(8,128)(2,1)S(1)}, bf16[8192,1,128]{2,0,1:T(8,128)(2,1)}, u32[]{:S(2)}) copy-start(bf16[8192,1,128]{2,0,1:T(8,128)(2,1)} %param.13) | copy-start | bytes 6291460
  38.8 1.6 %copy-start.1 = (bf16[8192,1,128]{2,0,1:T(8,128)(2,1)S(1)}, bf16[8192,1,128]{2,0,1:T(8,128)(2,1)}, u32[]{:S(2)}) copy-start(bf16[8192,1,128]{2,0,1:T(8,128)(2,1)} %param.17) | copy-start | bytes 6291460
  40.4 0.9 copy-start.3
  41.3 0.9 copy-start.4
  42.2 0.9 copy-start.5
  43.2 0.8 copy-start.6
  43.9 0.8 copy-start.7
  44.7 0.7 copy-start.8
  45.4 0.7 copy-start.9
  46.0 0.7 copy-start.10
  46.7 55.7 %copy-start.2 = (bf16[1024,128]{1,0:T(8,128)(2,1)S(1)}, bf16[1024,128]{1,0:T(8,128)(2,1)}, u32[]{:S(2)}) copy-start(bf16[1024,128]{1,0:T(8,128)(2,1)} %weight_ref.1) | copy-start | bytes 786436

commit v2 on v1

--- a/solution.py
+++ b/solution.py
@@ -20,8 +20,9 @@
 LOW = -1e30
 VMEM = pl.BlockSpec(memory_space=pltpu.VMEM)
 SMEM = pl.BlockSpec(memory_space=pltpu.SMEM)
-ANY = pl.BlockSpec(memory_space=pl.ANY)
-LIMIT = 48 * 1024 * 1024
+HBM = pl.BlockSpec(memory_space=pltpu.HBM)
+LIMIT = 60 * 1024 * 1024
+SMALL = 4 * 1024 * 1024
 
 
 def nt(a, b):
@@ -53,19 +54,26 @@
 
 def attend_kernel(
     own_ref,
+    q_ref,
+    len_hbm,
+    table_hbm,
+    own_q_hbm,
+    kscale_hbm,
+    chan_hbm,
+    outlier_hbm,
+    vscale_hbm,
+    kcodes_hbm,
+    vcodes_hbm,
+    skeys_hbm,
+    svalues_hbm,
+    out_ref,
     len_ref,
     table_ref,
-    q_ref,
     own_q_ref,
     kscale_ref,
     chan_ref,
     outlier_ref,
     vscale_ref,
-    kcodes_hbm,
-    vcodes_hbm,
-    skeys_hbm,
-    svalues_hbm,
-    out_ref,
     kbuf,
     vbuf,
     skbuf,
@@ -76,7 +84,7 @@
     acc,
     ksem,
     vsem,
-    ssem,
+    sem,
 ):
     keys = kbuf.shape[0]
     blocks = keys // BLOCK
@@ -87,18 +95,40 @@
         rows = pl.ds(pl.multiple_of(i * BLOCK, BLOCK), BLOCK)
         return pltpu.make_async_copy(hbm.at[rows, :], buf.at[rows, :], sem.at[i])
 
+    first = [
+        pltpu.make_async_copy(source, target, sem.at[n])
+        for n, (source, target) in enumerate(
+            ((kscale_hbm, kscale_ref), (chan_hbm, chan_ref), (outlier_hbm, outlier_ref))
+        )
+    ]
+    second = [
+        pltpu.make_async_copy(source, target, sem.at[3 + n])
+        for n, (source, target) in enumerate(
+            (
+                (vscale_hbm, vscale_ref),
+                (own_q_hbm, own_q_ref),
+                (skeys_hbm, skbuf),
+                (svalues_hbm, svbuf),
+                (len_hbm, len_ref),
+                (table_hbm, table_ref),
+            )
+        )
+    ]
+    for copy in first:
+        copy.start()
     for i in range(blocks):
         chunk(kcodes_hbm, kbuf, ksem, i).start()
-    skeys = pltpu.make_async_copy(skeys_hbm, skbuf, ssem.at[0])
-    svalues = pltpu.make_async_copy(svalues_hbm, svbuf, ssem.at[1])
-    skeys.start()
-    svalues.start()
+    for copy in second:
+        copy.start()
     for i in range(blocks):
         chunk(vcodes_hbm, vbuf, vsem, i).start()
 
     peak[...] = jnp.full(peak.shape, LOW, F32)
     page_lane = lax.broadcasted_iota(jnp.int32, chan_ref.shape, 1)
     channel = lax.broadcasted_iota(jnp.int32, (HEADS, LANES), 1)
+
+    for copy in first:
+        copy.wait()
 
     @pl.loop(0, blocks)
     def score_block(i):
@@ -130,6 +160,8 @@
     )
     total[...] = jnp.zeros(total.shape, F32)
     acc[...] = jnp.zeros(acc.shape, F32)
+    for copy in second:
+        copy.wait()
 
     @pl.loop(0, blocks)
     def value_block(i):
@@ -155,8 +187,6 @@
 
     total[...] = jnp.broadcast_to(jnp.sum(total[...], axis=1, keepdims=True), total.shape)
 
-    skeys.wait()
-    svalues.wait()
     own = pl.ds(pl.multiple_of(own_ref[0] * HEADS, HEADS), HEADS)
     live = len_ref[0]
     place = lax.broadcasted_iota(jnp.int32, (HEADS, PAGE), 1)
@@ -184,11 +214,18 @@
     total[own, :] = sums
     acc[own, :] = weighted
 
-    for z in range(queries // SPLIT):
-        rows = slice(z * SPLIT, (z + 1) * SPLIT)
-        out_ref[z, :SPLIT, :] = (acc[rows, :] / total[rows, :]).astype(BF16)
-        stat = split_rows(to_lanes(peak[rows, :] + jnp.log2(total[rows, :])))
-        out_ref[z, SPLIT:, :] = jnp.broadcast_to(stat, (STATS, LANES))
+    pieces = out_ref.shape[0]
+    stride = queries // SPLIT * HEADS
+    for c in range(pieces):
+        rows = [
+            slice(u * stride + c * HEADS, u * stride + (c + 1) * HEADS)
+            for u in range(SPLIT // HEADS)
+        ]
+        part = [acc[r, :] / total[r, :] for r in rows]
+        logs = [peak[r, :] + jnp.log2(total[r, :]) for r in rows]
+        out_ref[c, :SPLIT, :] = jnp.concatenate(part, axis=0).astype(BF16)
+        stat = split_rows(to_lanes(jnp.concatenate(logs, axis=0)))
+        out_ref[c, SPLIT:, :] = jnp.broadcast_to(stat, (STATS, LANES))
 
 
 def merge_kernel(in_ref, out_ref):
@@ -214,8 +251,11 @@
 
 def project_kernel(in_ref, weight_ref, out_ref, wide):
     blocks = in_ref.shape[0]
-    for z in range(blocks):
-        wide[z * SPLIT : (z + 1) * SPLIT, :] = in_ref[z].astype(F32)
+    for c in range(blocks):
+        block = in_ref[c].astype(F32)
+        for u in range(SPLIT // HEADS):
+            first = (u * blocks + c) * HEADS
+            wide[first : first + HEADS, :] = block[u * HEADS : (u + 1) * HEADS]
     samples = blocks * SPLIT // HEADS
     result = jnp.zeros((samples, LANES), F32)
     for h in range(HEADS):
@@ -252,7 +292,6 @@
     suffix_values,
     page_table,
     suffix_len,
-    depth,
 ):
     rows = all_queries.shape[0]
     keys = key_codes.shape[0]
@@ -260,10 +299,17 @@
     params = pltpu.CompilerParams(vmem_limit_bytes=LIMIT)
     return pl.pallas_call(
         attend_kernel,
-        out_shape=jax.ShapeDtypeStruct((depth, SPLIT + STATS, LANES), BF16),
-        in_specs=[SMEM] * 3 + [VMEM] * 6 + [ANY] * 4,
+        out_shape=jax.ShapeDtypeStruct((rows // SPLIT, SPLIT + STATS, LANES), BF16),
+        in_specs=[SMEM, VMEM] + [HBM] * 11,
         out_specs=VMEM,
         scratch_shapes=[
+            pltpu.SMEM(suffix_len.shape, jnp.int32),
+            pltpu.SMEM(page_table.shape, jnp.int32),
+            pltpu.VMEM(queries.shape, BF16),
+            pltpu.VMEM(key_scale.shape, F32),
+            pltpu.VMEM((HEADS, keys // PAGE), jnp.int32),
+            pltpu.VMEM((HEADS, keys), BF16),
+            pltpu.VMEM(value_scale.shape, F32),
             pltpu.VMEM((keys, LANES), BF16),
             pltpu.VMEM((keys, LANES), BF16),
             pltpu.VMEM((pools, PAGE, LANES), BF16),
@@ -274,15 +320,15 @@
             pltpu.VMEM((rows, LANES), F32),
             pltpu.SemaphoreType.DMA((keys // BLOCK,)),
             pltpu.SemaphoreType.DMA((keys // BLOCK,)),
-            pltpu.SemaphoreType.DMA((2,)),
+            pltpu.SemaphoreType.DMA((9,)),
         ],
         compiler_params=params,
         name="attend",
     )(
         own,
+        all_queries,
         suffix_len,
         page_table,
-        all_queries,
         queries,
         key_scale,
         outlier_chan.reshape(-1, HEADS).T,
@@ -309,12 +355,12 @@
     suffix_len,
     out_weight,
 ):
-    depth, width = lax.axis_size("z"), lax.axis_size("y")
-    samples = depth * width
+    seq, near, far = ("zh", "zl", "y"), ("zl", "y"), "zh"
+    samples = lax.axis_size(seq)
     queries = queries.reshape(HEADS, LANES)
-    all_queries = spread(spread(queries, "y"), "z").reshape(samples * HEADS, LANES)
-    own = (lax.axis_index("z") * width + lax.axis_index("y")).astype(jnp.int32).reshape(1)
-    params = pltpu.CompilerParams(vmem_limit_bytes=LIMIT)
+    all_queries = spread(queries, seq).reshape(samples * HEADS, LANES)
+    own = lax.axis_index(seq).astype(jnp.int32).reshape(1)
+    params = pltpu.CompilerParams(vmem_limit_bytes=SMALL)
     partial = attend(
         own,
         all_queries,
@@ -329,27 +375,26 @@
         suffix_values,
         page_table,
         suffix_len,
-        depth,
     )
-    partial = lax.all_to_all(partial, "z", 0, 0)
+    partial = lax.all_to_all(partial, near, 0, 0)
     partial = pl.pallas_call(
         merge_kernel,
-        out_shape=jax.ShapeDtypeStruct((width, SPLIT + STATS, LANES), BF16),
+        out_shape=jax.ShapeDtypeStruct((lax.axis_size(far), SPLIT + STATS, LANES), BF16),
         in_specs=[VMEM],
         out_specs=VMEM,
         compiler_params=params,
-        name="merge_z",
+        name="merge_near",
     )(partial)
-    partial = lax.all_to_all(partial, "y", 0, 0)
+    partial = lax.all_to_all(partial, far, 0, 0)
     attention = pl.pallas_call(
         merge_kernel,
-        out_shape=jax.ShapeDtypeStruct((depth, SPLIT, LANES), BF16),
+        out_shape=jax.ShapeDtypeStruct((lax.axis_size(near), SPLIT, LANES), BF16),
         in_specs=[VMEM],
         out_specs=VMEM,
         compiler_params=params,
-        name="merge_y",
+        name="merge_far",
     )(partial)
-    attention = lax.all_to_all(attention, "z", 0, 0)
+    attention = lax.all_to_all(attention, near, 0, 0)
     product = pl.pallas_call(
         project_kernel,
         out_shape=jax.ShapeDtypeStruct((samples, LANES), BF16),
@@ -372,8 +417,8 @@
 
 
 def solution(mesh):
-    grid = Mesh(mesh.devices.reshape(16, 4, 4, 2), ("z", "y", "x", "core"))
-    seq, tp = ("z", "y"), ("x", "core")
+    grid = Mesh(mesh.devices.reshape(4, 4, 4, 4, 2), ("zh", "zl", "y", "x", "core"))
+    seq, tp = ("zh", "zl", "y"), ("x", "core")
     return jax.shard_map(
         shards,
         mesh=grid,

time: 118 us -> 106 us (0.90)
  blocking collectives: 65.8 us -> 54 us
  local copies, waits for them, and re-layouts: 10.8 us -> 2 us
  starting transfers between devices: 14.9 us -> 19.3 us
  waiting for transfers between devices: 11.4 us -> 14.2 us
  Pallas kernels: 14.1 us -> 15.8 us
    all_to_all x4 -> x3, blocking collectives: 51.3 us -> 39.5 us  [the longest x1 16.4 us: shards(): partial = lax.all_to_all(partial, far, 0, 0)]
    unnamed x22 -> x4, local copies, waits for them, and re-layouts: 9.43 us -> 0.66 us
    all_to_all x1, starting transfers between devices: 14.9 us -> 19.3 us  [spread(): return lax.all_to_all(copies, axis, 0, 0)]
    all_to_all x1, waiting for transfers between devices: 11.4 us -> 14.2 us  [spread(): return lax.all_to_all(copies, axis, 0, 0)]
    pallas_call x3, Pallas kernels: 13.3 us -> 15 us  [the longest x1 14.7 us: attend(): pl.pallas_call(attend_kernel, out_shape=jax.ShapeDtypeStruct((rows // SPL...]
where the time goes in v2:
time: 106 us
  blocking collectives  54 us (51%)
  starting transfers between devices  19.3 us (18%)
  Pallas kernels  15.8 us (15%)
  waiting for transfers between devices  14.2 us (13%)
  local copies, waits for them, and re-layouts  2 us (2%)
    all_to_all x1, starting transfers between devices, spread(): return lax.all_to_all(copies, axis, 0, 0)  19.3 us
    all_to_all x1, blocking collectives, shards(): partial = lax.all_to_all(partial, far, 0, 0)  16.4 us
    pallas_call x1, Pallas kernels, attend(): pl.pallas_call(attend_kernel, out_shape=jax.ShapeDtypeStruct((rows // SPL...  14.7 us
    all_to_all x1, blocking collectives, shards(): lax.all_to_all(product.reshape(tp, samples // tp, LANES), ('x', 'core'),...  14.4 us
    all_to_all x1, waiting for transfers between devices, spread(): return lax.all_to_all(copies, axis, 0, 0)  14.2 us
    all_to_all x1, blocking collectives, shards(): partial = lax.all_to_all(partial, near, 0, 0)  12.6 us
    all_to_all x1, blocking collectives, shards(): attention = lax.all_to_all(attention, near, 0, 0)  10.5 us
  transfers between devices with their start and end apart: 1, of which 1 were waited for; matrix products, arithmetic and copies ran while one was open for 0% of the time, Pallas kernels for 0%

profile of v2, /device:TPU:1, one launch (start us, length us, event | category | flops | bytes accessed | tf_op | source)
XLA Modules:
  0.0 106.0 jit_solution(1518591745190033251)
XLA Ops:
  0.0 1.3 %broadcast_in_dim.8 = bf16[64,8,128]{2,1,0:T(8,128)(2,1)} broadcast(bf16[8,128]{1,0:T(8,128)(2,1)} %bitcast.21), dimensions={1,2} | broadcast | bytes 133120 | tf_op jit(solution)/shard_map/broadcast_in_dim | solution.py:277
  1.3 19.3 %all-to-all-start = ((bf16[64,8,128]{2,1,0:T(8,128)(2,1)}), bf16[64,8,128]{2,1,0:T(8,128)(2,1)S(1)}, u32[]{:S(2)}, u32[]{:S(2)}) async-start(bf16[64,8,128]{2,1,0:T(8,128)(2,1)} %broadcast_in_dim.8), calls=%async_computation | async-start | bytes 262144 | tf_op jit(solution)/shard_map/all_to_all | solution.py:278
  21.3 14.2 %all-to-all-done = bf16[64,8,128]{2,1,0:T(8,128)(2,1)S(1)} async-done(((bf16[64,8,128]{2,1,0:T(8,128)(2,1)}), bf16[64,8,128]{2,1,0:T(8,128)(2,1)S(1)}, u32[]{:S(2)}, u32[]{:S(2)}) %all-to-all-start) | async-done | bytes 131104 | tf_op jit(solution)/shard_map/all_to_all | solution.py:278
  35.5 0.0 copy-start.1
  35.5 0.7 copy-done.1
  36.2 0.0 copy-start
  36.2 14.7 %attend.1 = bf16[16,48,128]{2,1,0:T(8,128)(2,1)} custom-call(s32[1]{0:T(128)} %bitcast.own_ref, bf16[512,128]{1,0:T(8,128)(2,1)} %bitcast.17, s32[1]{0:T(128)S(6)} %copy.13.len_hbm, s32[1,4]{1,0:T(1,128)} %table_hbm.1, bf16[8,128]{1,0:T(8,128)(2,1)} %bitcast.22, f32[64,1,128]{2,1,0:T(1,128)} %kscale_hbm.1, s32[8,64]{1,0:T(8,128)} %bitcast.23, ...), custom_call_target="tpu_custom_call" | custom-call | tf_op jit(solution)/shard_map/attend/pallas_call | solution.py:300
  50.9 12.6 %all_to_all.25.in_ref = bf16[16,48,128]{2,1,0:T(8,128)(2,1)S(1)} all-to-all(bf16[16,48,128]{2,1,0:T(8,128)(2,1)} %attend.1), channel_id=1, replica_groups=mesh['zh'=4,'zl'=4,'y'=4,'x'=4,'core'=2] {'zl','y'}, dimensions={0} | all-to-all | bytes 393216 | tf_op jit(solution)/shard_map/all_to_all | solution.py:379
  63.5 0.2 merge_near.1
  63.8 16.4 %all_to_all.26.in_ref = bf16[4,48,128]{2,1,0:T(8,128)(2,1)S(1)} all-to-all(bf16[4,48,128]{2,1,0:T(8,128)(2,1)S(1)} %merge_near.1), channel_id=1, replica_groups=mesh['zh'=4,'zl'=4,'y'=4,'x'=4,'core'=2] {'zh'}, dimensions={0} | all-to-all | bytes 98304 | tf_op jit(solution)/shard_map/all_to_all | solution.py:388
  80.1 0.1 merge_far.1
  80.3 10.5 %all_to_all.27.in_ref = bf16[16,32,128]{2,1,0:T(8,128)(2,1)S(1)} all-to-all(bf16[16,32,128]{2,1,0:T(8,128)(2,1)S(1)} %merge_far.1), channel_id=1, replica_groups=mesh['zh'=4,'zl'=4,'y'=4,'x'=4,'core'=2] {'zl','y'}, dimensions={0} | all-to-all | bytes 262144 | tf_op jit(solution)/shard_map/all_to_all | solution.py:397
  90.8 0.0 copy-done
  90.8 0.2 project.1
  91.0 14.4 %all_to_all.28.in_ref = bf16[8,8,128]{2,1,0:T(8,128)(2,1)S(1)} all-to-all(bf16[8,8,128]{2,1,0:T(8,128)(2,1)S(1)} %bitcast.14), channel_id=1, replica_groups=mesh['zh'=4,'zl'=4,'y'=4,'x'=4,'core'=2] {'x','core'}, dimensions={0} | all-to-all | bytes 32768 | tf_op jit(solution)/shard_map/all_to_all | solution.py:408
  105.4 0.6 sum_tp.1
Async XLA Ops:
  1.3 34.2 %all-to-all-start = ((bf16[64,8,128]{2,1,0:T(8,128)(2,1)}), bf16[64,8,128]{2,1,0:T(8,128)(2,1)S(1)}, u32[]{:S(2)}, u32[]{:S(2)}) async-start(bf16[64,8,128]{2,1,0:T(8,128)(2,1)} %broadcast_in_dim.8), calls=%async_computation | async-start | bytes 262144 | tf_op jit(solution)/shard_map/all_to_all | solution.py:278
  35.5 0.7 copy-start.1
  36.2 54.6 %copy-start = (bf16[1024,128]{1,0:T(8,128)(2,1)S(1)}, bf16[1024,128]{1,0:T(8,128)(2,1)}, u32[]{:S(2)}) copy-start(bf16[1024,128]{1,0:T(8,128)(2,1)} %weight_ref.1) | copy-start | bytes 786436

commit v3 on v2

--- a/solution.py
+++ b/solution.py
@@ -358,8 +358,41 @@
     seq, near, far = ("zh", "zl", "y"), ("zl", "y"), "zh"
     samples = lax.axis_size(seq)
     queries = queries.reshape(HEADS, LANES)
+    own = lax.axis_index(seq).astype(jnp.int32).reshape(1)
     all_queries = spread(queries, seq).reshape(samples * HEADS, LANES)
-    own = lax.axis_index(seq).astype(jnp.int32).reshape(1)
+    (
+        own,
+        queries,
+        all_queries,
+        key_codes,
+        key_scale,
+        outlier_chan,
+        outlier_val,
+        value_codes,
+        value_scale,
+        suffix_keys,
+        suffix_values,
+        page_table,
+        suffix_len,
+        out_weight,
+    ) = lax.optimization_barrier(
+        (
+            own,
+            queries,
+            all_queries,
+            key_codes,
+            key_scale,
+            outlier_chan,
+            outlier_val,
+            value_codes,
+            value_scale,
+            suffix_keys,
+            suffix_values,
+            page_table,
+            suffix_len,
+            out_weight,
+        )
+    )
     params = pltpu.CompilerParams(vmem_limit_bytes=SMALL)
     partial = attend(
         own,

time: 106 us -> 106 us (level)
  no operation moved by 1% of the time
where the time goes in v3:
time: 106 us
  blocking collectives  54 us (51%)
  starting transfers between devices  19.3 us (18%)
  Pallas kernels  15.8 us (15%)
  waiting for transfers between devices  14.2 us (13%)
  local copies, waits for them, and re-layouts  2 us (2%)
    all_to_all x1, starting transfers between devices, spread(): return lax.all_to_all(copies, axis, 0, 0)  19.3 us
    all_to_all x1, blocking collectives, shards(): partial = lax.all_to_all(partial, far, 0, 0)  16.4 us
    pallas_call x1, Pallas kernels, attend(): pl.pallas_call(attend_kernel, out_shape=jax.ShapeDtypeStruct((rows // SPL...  14.7 us
    all_to_all x1, blocking collectives, shards(): lax.all_to_all(product.reshape(tp, samples // tp, LANES), ('x', 'core'),...  14.4 us
    all_to_all x1, waiting for transfers between devices, spread(): return lax.all_to_all(copies, axis, 0, 0)  14.2 us
    all_to_all x1, blocking collectives, shards(): partial = lax.all_to_all(partial, near, 0, 0)  12.6 us
    all_to_all x1, blocking collectives, shards(): attention = lax.all_to_all(attention, near, 0, 0)  10.5 us
  transfers between devices with their start and end apart: 1, of which 1 were waited for; matrix products, arithmetic and copies ran while one was open for 0% of the time, Pallas kernels for 0%

profile of v3, /device:TPU:1, one launch (start us, length us, event | category | flops | bytes accessed | tf_op | source)
XLA Modules:
  0.0 106.0 jit_solution(1518591745190033251)
XLA Ops:
  0.0 1.3 %broadcast_in_dim.2 = bf16[64,8,128]{2,1,0:T(8,128)(2,1)} broadcast(bf16[8,128]{1,0:T(8,128)(2,1)} %bitcast.21), dimensions={1,2} | broadcast | bytes 133120 | tf_op jit(solution)/shard_map/broadcast_in_dim | solution.py:277
  1.3 19.3 %all-to-all-start = ((bf16[64,8,128]{2,1,0:T(8,128)(2,1)}), bf16[64,8,128]{2,1,0:T(8,128)(2,1)S(1)}, u32[]{:S(2)}, u32[]{:S(2)}) async-start(bf16[64,8,128]{2,1,0:T(8,128)(2,1)} %broadcast_in_dim.2), calls=%async_computation | async-start | bytes 262144 | tf_op jit(solution)/shard_map/all_to_all | solution.py:278
  21.3 14.2 %all-to-all-done = bf16[64,8,128]{2,1,0:T(8,128)(2,1)S(1)} async-done(((bf16[64,8,128]{2,1,0:T(8,128)(2,1)}), bf16[64,8,128]{2,1,0:T(8,128)(2,1)S(1)}, u32[]{:S(2)}, u32[]{:S(2)}) %all-to-all-start) | async-done | bytes 131104 | tf_op jit(solution)/shard_map/all_to_all | solution.py:278
  35.5 0.0 copy-start.1
  35.5 0.7 copy-done.1
  36.2 0.0 copy-start
  36.2 14.7 %attend.1 = bf16[16,48,128]{2,1,0:T(8,128)(2,1)} custom-call(s32[1]{0:T(128)} %bitcast.own_ref, bf16[512,128]{1,0:T(8,128)(2,1)} %bitcast.17, s32[1]{0:T(128)S(6)} %copy.13.len_hbm, s32[1,4]{1,0:T(1,128)} %table_hbm, bf16[8,128]{1,0:T(8,128)(2,1)} %bitcast.22, f32[64,1,128]{2,1,0:T(1,128)} %kscale_hbm, s32[8,64]{1,0:T(8,128)} %bitcast.23, ...), custom_call_target="tpu_custom_call" | custom-call | tf_op jit(solution)/shard_map/attend/pallas_call | solution.py:300
  50.9 12.6 %all_to_all.25.in_ref = bf16[16,48,128]{2,1,0:T(8,128)(2,1)S(1)} all-to-all(bf16[16,48,128]{2,1,0:T(8,128)(2,1)} %attend.1), channel_id=1, replica_groups=mesh['zh'=4,'zl'=4,'y'=4,'x'=4,'core'=2] {'zl','y'}, dimensions={0} | all-to-all | bytes 393216 | tf_op jit(solution)/shard_map/all_to_all | solution.py:412
  63.5 0.2 merge_near.1
  63.8 16.4 %all_to_all.26.in_ref = bf16[4,48,128]{2,1,0:T(8,128)(2,1)S(1)} all-to-all(bf16[4,48,128]{2,1,0:T(8,128)(2,1)S(1)} %merge_near.1), channel_id=1, replica_groups=mesh['zh'=4,'zl'=4,'y'=4,'x'=4,'core'=2] {'zh'}, dimensions={0} | all-to-all | bytes 98304 | tf_op jit(solution)/shard_map/all_to_all | solution.py:421
  80.1 0.1 merge_far.1
  80.3 10.5 %all_to_all.27.in_ref = bf16[16,32,128]{2,1,0:T(8,128)(2,1)S(1)} all-to-all(bf16[16,32,128]{2,1,0:T(8,128)(2,1)S(1)} %merge_far.1), channel_id=1, replica_groups=mesh['zh'=4,'zl'=4,'y'=4,'x'=4,'core'=2] {'zl','y'}, dimensions={0} | all-to-all | bytes 262144 | tf_op jit(solution)/shard_map/all_to_all | solution.py:430
  90.8 0.0 copy-done
  90.8 0.2 project.1
  91.0 14.4 %all_to_all.28.in_ref = bf16[8,8,128]{2,1,0:T(8,128)(2,1)S(1)} all-to-all(bf16[8,8,128]{2,1,0:T(8,128)(2,1)S(1)} %bitcast.14), channel_id=1, replica_groups=mesh['zh'=4,'zl'=4,'y'=4,'x'=4,'core'=2] {'x','core'}, dimensions={0} | all-to-all | bytes 32768 | tf_op jit(solution)/shard_map/all_to_all | solution.py:441
  105.4 0.6 sum_tp.1
Async XLA Ops:
  1.3 34.2 %all-to-all-start = ((bf16[64,8,128]{2,1,0:T(8,128)(2,1)}), bf16[64,8,128]{2,1,0:T(8,128)(2,1)S(1)}, u32[]{:S(2)}, u32[]{:S(2)}) async-start(bf16[64,8,128]{2,1,0:T(8,128)(2,1)} %broadcast_in_dim.2), calls=%async_computation | async-start | bytes 262144 | tf_op jit(solution)/shard_map/all_to_all | solution.py:278
  35.5 0.7 copy-start.1
  36.2 54.6 %copy-start = (bf16[1024,128]{1,0:T(8,128)(2,1)S(1)}, bf16[1024,128]{1,0:T(8,128)(2,1)}, u32[]{:S(2)}) copy-start(bf16[1024,128]{1,0:T(8,128)(2,1)} %weight_ref) | copy-start | bytes 786436

commit v4 on v2

--- a/solution.py
+++ b/solution.py
@@ -15,13 +15,16 @@
 PAGE = 128
 TILE = 256
 BLOCK = 1024
+PAGES = BLOCK // PAGE
+SCORE_SCALE = math.log2(math.e) / math.sqrt(LANES)
 SPLIT = 32
 STATS = 16
 LOW = -1e30
 VMEM = pl.BlockSpec(memory_space=pltpu.VMEM)
 SMEM = pl.BlockSpec(memory_space=pltpu.SMEM)
 HBM = pl.BlockSpec(memory_space=pltpu.HBM)
-LIMIT = 60 * 1024 * 1024
+PREPARE_LIMIT = 57 * 1024 * 1024
+ATTEND_LIMIT = 57 * 1024 * 1024
 SMALL = 4 * 1024 * 1024
 
 
@@ -52,9 +55,7 @@
     return jnp.sum(jnp.where(lane % SPLIT == row, wide, 0.0), axis=1, keepdims=True)
 
 
-def attend_kernel(
-    own_ref,
-    q_ref,
+def prepare_kernel(
     len_hbm,
     table_hbm,
     own_q_hbm,
@@ -66,7 +67,9 @@
     vcodes_hbm,
     skeys_hbm,
     svalues_hbm,
-    out_ref,
+    keys_ref,
+    values_ref,
+    own_ref,
     len_ref,
     table_ref,
     own_q_ref,
@@ -74,37 +77,26 @@
     chan_ref,
     outlier_ref,
     vscale_ref,
-    kbuf,
-    vbuf,
     skbuf,
     svbuf,
-    scores,
-    peak,
-    total,
-    acc,
+    onehot,
     ksem,
     vsem,
     sem,
 ):
-    keys = kbuf.shape[0]
-    blocks = keys // BLOCK
-    queries = q_ref.shape[0]
-    score_scale = math.log2(math.e) / math.sqrt(LANES)
-
-    def chunk(hbm, buf, sem, i):
+    blocks = keys_ref.shape[0] // BLOCK
+
+    def chunk(hbm, buf, sems, i):
         rows = pl.ds(pl.multiple_of(i * BLOCK, BLOCK), BLOCK)
-        return pltpu.make_async_copy(hbm.at[rows, :], buf.at[rows, :], sem.at[i])
-
-    first = [
+        return pltpu.make_async_copy(hbm.at[rows, :], buf.at[rows, :], sems.at[i])
+
+    small = [
         pltpu.make_async_copy(source, target, sem.at[n])
         for n, (source, target) in enumerate(
-            ((kscale_hbm, kscale_ref), (chan_hbm, chan_ref), (outlier_hbm, outlier_ref))
-        )
-    ]
-    second = [
-        pltpu.make_async_copy(source, target, sem.at[3 + n])
-        for n, (source, target) in enumerate(
             (
+                (chan_hbm, chan_ref),
+                (outlier_hbm, outlier_ref),
+                (kscale_hbm, kscale_ref),
                 (vscale_hbm, vscale_ref),
                 (own_q_hbm, own_q_ref),
                 (skeys_hbm, skbuf),
@@ -114,105 +106,146 @@
             )
         )
     ]
-    for copy in first:
+    for copy in small:
         copy.start()
     for i in range(blocks):
-        chunk(kcodes_hbm, kbuf, ksem, i).start()
-    for copy in second:
-        copy.start()
+        chunk(kcodes_hbm, keys_ref, ksem, i).start()
     for i in range(blocks):
-        chunk(vcodes_hbm, vbuf, vsem, i).start()
-
-    peak[...] = jnp.full(peak.shape, LOW, F32)
-    page_lane = lax.broadcasted_iota(jnp.int32, chan_ref.shape, 1)
-    channel = lax.broadcasted_iota(jnp.int32, (HEADS, LANES), 1)
-
-    for copy in first:
+        chunk(vcodes_hbm, values_ref, vsem, i).start()
+    for copy in small:
         copy.wait()
 
-    @pl.loop(0, blocks)
-    def score_block(i):
-        chunk(kcodes_hbm, kbuf, ksem, i).wait()
-        running = peak[...]
-        for j in range(BLOCK // TILE):
-            parts = []
-            for p in range(TILE // PAGE):
-                page = i * (BLOCK // PAGE) + j * (TILE // PAGE) + p
-                rows = pl.ds(pl.multiple_of(page * PAGE, PAGE), PAGE)
-                chosen = jnp.sum(
-                    jnp.where(page_lane == page, chan_ref[...], 0), axis=1, keepdims=True
-                )
-                onehot = (channel == chosen).astype(BF16)
-                correction = lax.dot_general(
-                    outlier_ref[:, rows],
-                    onehot,
-                    (((0,), (0,)), ((), ())),
-                    preferred_element_type=F32,
-                )
-                parts.append((kbuf[rows, :].astype(F32) * kscale_ref[page] + correction).astype(BF16))
-            tile = nt(q_ref[...], jnp.concatenate(parts, axis=0))
-            scores[i * (BLOCK // TILE) + j] = tile
-            running = jnp.maximum(running, jnp.maximum(tile[:, :LANES], tile[:, LANES:]))
-        peak[...] = running
-
-    peak[...] = jnp.broadcast_to(
-        jnp.max(peak[...], axis=1, keepdims=True) * score_scale, peak.shape
-    )
-    total[...] = jnp.zeros(total.shape, F32)
-    acc[...] = jnp.zeros(acc.shape, F32)
-    for copy in second:
-        copy.wait()
-
-    @pl.loop(0, blocks)
-    def value_block(i):
-        chunk(vcodes_hbm, vbuf, vsem, i).wait()
-        running = total[...]
-        top = peak[...]
-        weights, values = [], []
-        for j in range(BLOCK // TILE):
-            for p in range(TILE // PAGE):
-                page = i * (BLOCK // PAGE) + j * (TILE // PAGE) + p
-                rows = pl.ds(pl.multiple_of(page * PAGE, PAGE), PAGE)
-                values.append((vbuf[rows, :].astype(F32) * vscale_ref[page]).astype(BF16))
-                part = scores[i * (BLOCK // TILE) + j, :, p * LANES : (p + 1) * LANES]
-                weight = jnp.exp2(part * score_scale - top)
-                running = running + weight
-                weights.append(weight.astype(BF16))
-        total[...] = running
-        acc[...] += jnp.dot(
-            jnp.concatenate(weights, axis=1),
-            jnp.concatenate(values, axis=0),
-            preferred_element_type=F32,
-        )
-
-    total[...] = jnp.broadcast_to(jnp.sum(total[...], axis=1, keepdims=True), total.shape)
-
-    own = pl.ds(pl.multiple_of(own_ref[0] * HEADS, HEADS), HEADS)
+    lane = lax.broadcasted_iota(jnp.int32, (HEADS, LANES), 1)
+    channels = chan_ref[...]
+    for page in range(onehot.shape[0]):
+        onehot[page] = (lane == channels[:, page : page + 1]).astype(F32)
+
     live = len_ref[0]
-    place = lax.broadcasted_iota(jnp.int32, (HEADS, PAGE), 1)
     own_scores = [
         jnp.where(
-            place + j * PAGE < live,
-            nt(own_q_ref[...], skbuf[table_ref[0, j]]) * score_scale,
+            lane + j * PAGE < live,
+            nt(own_q_ref[...], skbuf[table_ref[0, j]]) * SCORE_SCALE,
             LOW,
         )
         for j in range(skbuf.shape[0])
     ]
-    top = peak[own, :]
-    for part in own_scores:
-        top = jnp.maximum(top, jnp.max(part, axis=1, keepdims=True))
-    fade = jnp.exp2(peak[own, :] - top)
-    sums = total[own, :] * fade
-    weighted = acc[own, :] * fade
+    top = functools.reduce(jnp.maximum, own_scores)
+    top = jnp.max(top, axis=1, keepdims=True)
+    sums = jnp.zeros((HEADS, LANES), F32)
+    weighted = jnp.zeros((HEADS, LANES), F32)
     for j, part in enumerate(own_scores):
-        weight = jnp.where(place + j * PAGE < live, jnp.exp2(part - top), 0.0)
-        sums = sums + jnp.sum(weight, axis=1, keepdims=True)
+        weight = jnp.where(lane + j * PAGE < live, jnp.exp2(part - top), 0.0)
+        sums = sums + weight
         weighted = weighted + jnp.dot(
             weight.astype(BF16), svbuf[table_ref[0, j]], preferred_element_type=F32
         )
+    own_ref[0] = jnp.broadcast_to(top, (HEADS, LANES))
+    own_ref[1] = jnp.broadcast_to(jnp.sum(sums, axis=1, keepdims=True), (HEADS, LANES))
+    own_ref[2] = weighted
+    none = jnp.zeros((HEADS, LANES), F32)
+
+    @pl.loop(0, blocks)
+    def key_block(i):
+        chunk(kcodes_hbm, keys_ref, ksem, i).wait()
+        first_page = i * PAGES
+        slots = [
+            outlier_ref[:, pl.ds(pl.multiple_of((first_page + p) * PAGE, PAGE), PAGE)].astype(F32)
+            for p in range(PAGES)
+        ]
+        slots = jnp.concatenate(slots + [none] * (LANES // HEADS - PAGES), axis=0).T.astype(BF16)
+        chosen = []
+        for p in range(PAGES):
+            column = [none] * (LANES // HEADS)
+            column[p] = onehot[first_page + p]
+            chosen.append(jnp.concatenate(column, axis=0).astype(BF16))
+        correction = jnp.dot(slots, jnp.concatenate(chosen, axis=1), preferred_element_type=F32)
+        for p in range(PAGES):
+            rows = pl.ds(pl.multiple_of((first_page + p) * PAGE, PAGE), PAGE)
+            base = keys_ref[rows, :].astype(F32) * kscale_ref[first_page + p]
+            keys_ref[rows, :] = (base + correction[:, p * LANES : (p + 1) * LANES]).astype(BF16)
+
+    @pl.loop(0, blocks)
+    def value_block(i):
+        chunk(vcodes_hbm, values_ref, vsem, i).wait()
+        for p in range(PAGES):
+            rows = pl.ds(pl.multiple_of((i * PAGES + p) * PAGE, PAGE), PAGE)
+            values_ref[rows, :] = (
+                values_ref[rows, :].astype(F32) * vscale_ref[i * PAGES + p]
+            ).astype(BF16)
+
+
+def attend_kernel(
+    place_ref,
+    q_ref,
+    own_ref,
+    keys_hbm,
+    values_hbm,
+    out_ref,
+    keys_ref,
+    values_ref,
+    scores,
+    peak,
+    total,
+    acc,
+    ksem,
+    sem,
+):
+    load = pltpu.make_async_copy(values_hbm, values_ref, sem)
+
+    def chunk(i):
+        rows = pl.ds(pl.multiple_of(i * BLOCK, BLOCK), BLOCK)
+        return pltpu.make_async_copy(keys_hbm.at[rows, :], keys_ref.at[rows, :], ksem.at[i])
+
+    for i in range(keys_ref.shape[0] // BLOCK):
+        chunk(i).start()
+    load.start()
+    blocks = keys_ref.shape[0] // BLOCK
+    queries = q_ref.shape[0]
+    peak[...] = jnp.full(peak.shape, LOW, F32)
+
+    @pl.loop(0, blocks)
+    def score_block(i):
+        chunk(i).wait()
+        running = peak[...]
+        for j in range(BLOCK // TILE):
+            rows = pl.ds(pl.multiple_of(i * BLOCK + j * TILE, TILE), TILE)
+            tile = nt(q_ref[...], keys_ref[rows, :])
+            scores[i * (BLOCK // TILE) + j] = tile
+            running = jnp.maximum(running, jnp.maximum(tile[:, :LANES], tile[:, LANES:]))
+        peak[...] = running
+
+    peak[...] = jnp.broadcast_to(
+        jnp.max(peak[...], axis=1, keepdims=True) * SCORE_SCALE, peak.shape
+    )
+    total[...] = jnp.zeros(total.shape, F32)
+    acc[...] = jnp.zeros(acc.shape, F32)
+    load.wait()
+
+    @pl.loop(0, blocks)
+    def value_block(i):
+        running = total[...]
+        top = peak[...]
+        weights = []
+        for j in range(BLOCK // TILE):
+            for p in range(TILE // PAGE):
+                part = scores[i * (BLOCK // TILE) + j, :, p * LANES : (p + 1) * LANES]
+                weight = jnp.exp2(part * SCORE_SCALE - top)
+                running = running + weight
+                weights.append(weight.astype(BF16))
+        total[...] = running
+        rows = pl.ds(pl.multiple_of(i * BLOCK, BLOCK), BLOCK)
+        acc[...] += jnp.dot(
+            jnp.concatenate(weights, axis=1), values_ref[rows, :], preferred_element_type=F32
+        )
+
+    total[...] = jnp.broadcast_to(jnp.sum(total[...], axis=1, keepdims=True), total.shape)
+
+    own = pl.ds(pl.multiple_of(place_ref[0] * HEADS, HEADS), HEADS)
+    top = jnp.maximum(peak[own, :], own_ref[0])
+    fade, own_fade = jnp.exp2(peak[own, :] - top), jnp.exp2(own_ref[0] - top)
     peak[own, :] = top
-    total[own, :] = sums
-    acc[own, :] = weighted
+    total[own, :] = total[own, :] * fade + own_ref[1] * own_fade
+    acc[own, :] = acc[own, :] * fade + own_ref[2] * own_fade
 
     pieces = out_ref.shape[0]
     stride = queries // SPLIT * HEADS
@@ -278,9 +311,7 @@
     return lax.all_to_all(copies, axis, 0, 0)
 
 
-def attend(
-    own,
-    all_queries,
+def prepare(
     queries,
     key_codes,
     key_scale,
@@ -293,15 +324,17 @@
     page_table,
     suffix_len,
 ):
-    rows = all_queries.shape[0]
     keys = key_codes.shape[0]
     pools = suffix_keys.shape[0]
-    params = pltpu.CompilerParams(vmem_limit_bytes=LIMIT)
     return pl.pallas_call(
-        attend_kernel,
-        out_shape=jax.ShapeDtypeStruct((rows // SPLIT, SPLIT + STATS, LANES), BF16),
-        in_specs=[SMEM, VMEM] + [HBM] * 11,
-        out_specs=VMEM,
+        prepare_kernel,
+        out_shape=(
+            jax.ShapeDtypeStruct((keys, LANES), BF16),
+            jax.ShapeDtypeStruct((keys, LANES), BF16),
+            jax.ShapeDtypeStruct((3, HEADS, LANES), F32),
+        ),
+        in_specs=[HBM] * 11,
+        out_specs=(VMEM, VMEM, VMEM),
         scratch_shapes=[
             pltpu.SMEM(suffix_len.shape, jnp.int32),
             pltpu.SMEM(page_table.shape, jnp.int32),
@@ -310,23 +343,19 @@
             pltpu.VMEM((HEADS, keys // PAGE), jnp.int32),
             pltpu.VMEM((HEADS, keys), BF16),
             pltpu.VMEM(value_scale.shape, F32),
-            pltpu.VMEM((keys, LANES), BF16),
-            pltpu.VMEM((keys, LANES), BF16),
             pltpu.VMEM((pools, PAGE, LANES), BF16),
             pltpu.VMEM((pools, PAGE, LANES), BF16),
-            pltpu.VMEM((keys // TILE, rows, TILE), F32),
-            pltpu.VMEM((rows, LANES), F32),
-            pltpu.VMEM((rows, LANES), F32),
-            pltpu.VMEM((rows, LANES), F32),
+            pltpu.VMEM((keys // PAGE, HEADS, LANES), F32),
             pltpu.SemaphoreType.DMA((keys // BLOCK,)),
             pltpu.SemaphoreType.DMA((keys // BLOCK,)),
             pltpu.SemaphoreType.DMA((9,)),
         ],
-        compiler_params=params,
-        name="attend",
+        compiler_params=pltpu.CompilerParams(vmem_limit_bytes=PREPARE_LIMIT),
+        cost_estimate=pl.CostEstimate(
+            flops=2 * keys * LANES * LANES, bytes_accessed=10 * keys * LANES, transcendentals=0
+        ),
+        name="prepare",
     )(
-        own,
-        all_queries,
         suffix_len,
         page_table,
         queries,
@@ -339,6 +368,28 @@
         suffix_keys.reshape(pools, PAGE, LANES),
         suffix_values.reshape(pools, PAGE, LANES),
     )
+
+
+def attend(place, all_queries, keys, values, own):
+    rows = all_queries.shape[0]
+    return pl.pallas_call(
+        attend_kernel,
+        out_shape=jax.ShapeDtypeStruct((rows // SPLIT, SPLIT + STATS, LANES), BF16),
+        in_specs=[SMEM, VMEM, VMEM, HBM, HBM],
+        out_specs=VMEM,
+        scratch_shapes=[
+            pltpu.VMEM(keys.shape, BF16),
+            pltpu.VMEM(values.shape, BF16),
+            pltpu.VMEM((keys.shape[0] // TILE, rows, TILE), F32),
+            pltpu.VMEM((rows, LANES), F32),
+            pltpu.VMEM((rows, LANES), F32),
+            pltpu.VMEM((rows, LANES), F32),
+            pltpu.SemaphoreType.DMA((keys.shape[0] // BLOCK,)),
+            pltpu.SemaphoreType.DMA,
+        ],
+        compiler_params=pltpu.CompilerParams(vmem_limit_bytes=ATTEND_LIMIT),
+        name="attend",
+    )(place, all_queries, own, keys, values)
 
 
 def shards(
@@ -361,9 +412,7 @@
     all_queries = spread(queries, seq).reshape(samples * HEADS, LANES)
     own = lax.axis_index(seq).astype(jnp.int32).reshape(1)
     params = pltpu.CompilerParams(vmem_limit_bytes=SMALL)
-    partial = attend(
-        own,
-        all_queries,
+    prepared = prepare(
         queries,
         key_codes,
         key_scale,
@@ -376,6 +425,7 @@
         page_table,
         suffix_len,
     )
+    partial = attend(own, all_queries, *prepared)
     partial = lax.all_to_all(partial, near, 0, 0)
     partial = pl.pallas_call(
         merge_kernel,

time: 106 us -> 102 us (0.962)
  waiting for transfers between devices: 14.2 us -> 6.62 us
  Pallas kernels: 15.8 us -> 19.2 us
    all_to_all x1, waiting for transfers between devices: 14.2 us -> 6.62 us  [spread(): return lax.all_to_all(copies, axis, 0, 0)]
    pallas_call x0 -> x1, Pallas kernels: none -> 7.62 us  [prepare(): pl.pallas_call(prepare_kernel, out_shape=(jax.ShapeDtypeStruct((keys, LAN...]
    pallas_call x1, Pallas kernels: 14.7 us -> 10.5 us  [attend(): pl.pallas_call(attend_kernel, out_shape=jax.ShapeDtypeStruct((rows // SPL...]
  transfers between devices with their start and end apart: 1 -> 1, of which waited for: 1 -> 1; matrix products, arithmetic and copies ran while one was open for 0% -> 0% of each run, Pallas kernels for 0% -> 7%
where the time goes in v4:
time: 102 us
  blocking collectives  54 us (53%)
  starting transfers between devices  19.3 us (19%)
  Pallas kernels  19.2 us (19%)
  waiting for transfers between devices  6.62 us (6%)
  local copies, waits for them, and re-layouts  2.01 us (2%)
    all_to_all x1, starting transfers between devices, spread(): return lax.all_to_all(copies, axis, 0, 0)  19.3 us
    all_to_all x1, blocking collectives, shards(): partial = lax.all_to_all(partial, far, 0, 0)  16.4 us
    all_to_all x1, blocking collectives, shards(): lax.all_to_all(product.reshape(tp, samples // tp, LANES), ('x', 'core'),...  14.4 us
    all_to_all x1, blocking collectives, shards(): partial = lax.all_to_all(partial, near, 0, 0)  12.6 us
    all_to_all x1, blocking collectives, shards(): attention = lax.all_to_all(attention, near, 0, 0)  10.5 us
    pallas_call x1, Pallas kernels, attend(): pl.pallas_call(attend_kernel, out_shape=jax.ShapeDtypeStruct((rows // SPL...  10.5 us
    pallas_call x1, Pallas kernels, prepare(): pl.pallas_call(prepare_kernel, out_shape=(jax.ShapeDtypeStruct((keys, LAN...  7.62 us
    all_to_all x1, waiting for transfers between devices, spread(): return lax.all_to_all(copies, axis, 0, 0)  6.62 us
  transfers between devices with their start and end apart: 1, of which 1 were waited for; matrix products, arithmetic and copies ran while one was open for 0% of the time, Pallas kernels for 7%

profile of v4, /device:TPU:1, one launch (start us, length us, event | category | flops | bytes accessed | tf_op | source)
XLA Modules:
  0.0 101.8 jit_solution(10640424695352538194)
XLA Ops:
  0.0 1.3 %broadcast_in_dim.8 = bf16[64,8,128]{2,1,0:T(8,128)(2,1)} broadcast(bf16[8,128]{1,0:T(8,128)(2,1)} %bitcast.21), dimensions={1,2} | broadcast | bytes 133120 | tf_op jit(solution)/shard_map/broadcast_in_dim | solution.py:310
  1.3 19.3 %all-to-all-start = ((bf16[64,8,128]{2,1,0:T(8,128)(2,1)}), bf16[64,8,128]{2,1,0:T(8,128)(2,1)S(1)}, u32[]{:S(2)}, u32[]{:S(2)}) async-start(bf16[64,8,128]{2,1,0:T(8,128)(2,1)} %broadcast_in_dim.8), calls=%async_computation | async-start | bytes 262144 | tf_op jit(solution)/shard_map/all_to_all | solution.py:311
  21.3 7.6 %prepare.1 = (bf16[8192,128]{1,0:T(8,128)(2,1)}, bf16[8192,128]{1,0:T(8,128)(2,1)}, f32[3,8,128]{2,1,0:T(8,128)}) custom-call(s32[1]{0:T(128)S(6)} %copy.13.len_hbm, s32[1,4]{1,0:T(1,128)} %table_hbm.1, bf16[8,128]{1,0:T(8,128)(2,1)} %bitcast.22, f32[64,1,128]{2,1,0:T(1,128)} %kscale_hbm.1, s32[8,64]{1,0:T(8,128)} %bitcast.23, bf16[8,8192]{1,0:T(8,128)(2,1)} %bitcast.18, ...), custom_call_target="tpu_custom_call" | custom-call | flops 268435456 | bytes 10485760 | tf_op jit(solution)/shard_map/prepare/pallas_call | solution.py:329
  28.9 6.6 %all-to-all-done = bf16[64,8,128]{2,1,0:T(8,128)(2,1)S(1)} async-done(((bf16[64,8,128]{2,1,0:T(8,128)(2,1)}), bf16[64,8,128]{2,1,0:T(8,128)(2,1)S(1)}, u32[]{:S(2)}, u32[]{:S(2)}) %all-to-all-start) | async-done | bytes 131104 | tf_op jit(solution)/shard_map/all_to_all | solution.py:311
  35.5 0.0 copy-start.1
  35.5 0.7 copy-done.1
  36.2 0.0 copy-start
  36.2 10.5 %attend.1 = bf16[16,48,128]{2,1,0:T(8,128)(2,1)} custom-call(s32[1]{0:T(128)} %bitcast.place_ref, bf16[512,128]{1,0:T(8,128)(2,1)} %bitcast.17, f32[3,8,128]{2,1,0:T(8,128)} %get-tuple-element.8.own_ref, bf16[8192,128]{1,0:T(8,128)(2,1)} %get-tuple-element.9.keys_hbm, bf16[8192,128]{1,0:T(8,128)(2,1)} %get-tuple-element.10.values_hbm), custom_call_target="tpu_custom_call" | custom-call | tf_op jit(solution)/shard_map/attend/pallas_call | solution.py:375
  46.7 12.6 %all_to_all.25.in_ref = bf16[16,48,128]{2,1,0:T(8,128)(2,1)S(1)} all-to-all(bf16[16,48,128]{2,1,0:T(8,128)(2,1)} %attend.1), channel_id=1, replica_groups=mesh['zh'=4,'zl'=4,'y'=4,'x'=4,'core'=2] {'zl','y'}, dimensions={0} | all-to-all | bytes 393216 | tf_op jit(solution)/shard_map/all_to_all | solution.py:429
  59.3 0.2 merge_near.1
  59.6 16.4 %all_to_all.26.in_ref = bf16[4,48,128]{2,1,0:T(8,128)(2,1)S(1)} all-to-all(bf16[4,48,128]{2,1,0:T(8,128)(2,1)S(1)} %merge_near.1), channel_id=1, replica_groups=mesh['zh'=4,'zl'=4,'y'=4,'x'=4,'core'=2] {'zh'}, dimensions={0} | all-to-all | bytes 98304 | tf_op jit(solution)/shard_map/all_to_all | solution.py:438
  75.9 0.1 merge_far.1
  76.1 10.5 %all_to_all.27.in_ref = bf16[16,32,128]{2,1,0:T(8,128)(2,1)S(1)} all-to-all(bf16[16,32,128]{2,1,0:T(8,128)(2,1)S(1)} %merge_far.1), channel_id=1, replica_groups=mesh['zh'=4,'zl'=4,'y'=4,'x'=4,'core'=2] {'zl','y'}, dimensions={0} | all-to-all | bytes 262144 | tf_op jit(solution)/shard_map/all_to_all | solution.py:447
  86.6 0.0 copy-done
  86.6 0.2 project.1
  86.8 14.4 %all_to_all.28.in_ref = bf16[8,8,128]{2,1,0:T(8,128)(2,1)S(1)} all-to-all(bf16[8,8,128]{2,1,0:T(8,128)(2,1)S(1)} %bitcast.14), channel_id=1, replica_groups=mesh['zh'=4,'zl'=4,'y'=4,'x'=4,'core'=2] {'x','core'}, dimensions={0} | all-to-all | bytes 32768 | tf_op jit(solution)/shard_map/all_to_all | solution.py:458
  101.2 0.6 sum_tp.1
Async XLA Ops:
  1.3 34.2 %all-to-all-start = ((bf16[64,8,128]{2,1,0:T(8,128)(2,1)}), bf16[64,8,128]{2,1,0:T(8,128)(2,1)S(1)}, u32[]{:S(2)}, u32[]{:S(2)}) async-start(bf16[64,8,128]{2,1,0:T(8,128)(2,1)} %broadcast_in_dim.8), calls=%async_computation | async-start | bytes 262144 | tf_op jit(solution)/shard_map/all_to_all | solution.py:311
  35.5 0.7 copy-start.1
  36.2 50.4 %copy-start = (bf16[1024,128]{1,0:T(8,128)(2,1)S(1)}, bf16[1024,128]{1,0:T(8,128)(2,1)}, u32[]{:S(2)}) copy-start(bf16[1024,128]{1,0:T(8,128)(2,1)} %weight_ref.1) | copy-start | bytes 786436

commit v5 on v4

--- a/solution.py
+++ b/solution.py
@@ -15,6 +15,7 @@
 PAGE = 128
 TILE = 256
 BLOCK = 1024
+ROOM = 256
 PAGES = BLOCK // PAGE
 SCORE_SCALE = math.log2(math.e) / math.sqrt(LANES)
 SPLIT = 32
@@ -23,8 +24,8 @@
 VMEM = pl.BlockSpec(memory_space=pltpu.VMEM)
 SMEM = pl.BlockSpec(memory_space=pltpu.SMEM)
 HBM = pl.BlockSpec(memory_space=pltpu.HBM)
-PREPARE_LIMIT = 57 * 1024 * 1024
-ATTEND_LIMIT = 57 * 1024 * 1024
+PREPARE_LIMIT = 54 * 1024 * 1024
+ATTEND_LIMIT = 53 * 1024 * 1024
 SMALL = 4 * 1024 * 1024
 
 
@@ -67,9 +68,9 @@
     vcodes_hbm,
     skeys_hbm,
     svalues_hbm,
-    keys_ref,
-    values_ref,
-    own_ref,
+    keys_hbm,
+    values_hbm,
+    own_hbm,
     len_ref,
     table_ref,
     own_q_ref,
@@ -79,16 +80,23 @@
     vscale_ref,
     skbuf,
     svbuf,
+    kbuf,
+    vbuf,
+    own_ref,
     onehot,
     ksem,
     vsem,
+    kout,
+    vout,
     sem,
 ):
-    blocks = keys_ref.shape[0] // BLOCK
+    blocks = kbuf.shape[0] // BLOCK
+
+    def block_rows(i):
+        return pl.ds(pl.multiple_of(i * BLOCK, BLOCK), BLOCK)
 
     def chunk(hbm, buf, sems, i):
-        rows = pl.ds(pl.multiple_of(i * BLOCK, BLOCK), BLOCK)
-        return pltpu.make_async_copy(hbm.at[rows, :], buf.at[rows, :], sems.at[i])
+        return pltpu.make_async_copy(hbm.at[block_rows(i), :], buf.at[block_rows(i), :], sems.at[i])
 
     small = [
         pltpu.make_async_copy(source, target, sem.at[n])
@@ -106,20 +114,50 @@
             )
         )
     ]
-    for copy in small:
+    result = pltpu.make_async_copy(own_ref, own_hbm.at[0], sem.at[len(small)])
+    for copy in small[:3]:
         copy.start()
     for i in range(blocks):
-        chunk(kcodes_hbm, keys_ref, ksem, i).start()
+        chunk(kcodes_hbm, kbuf, ksem, i).start()
+    for copy in small[3:]:
+        copy.start()
     for i in range(blocks):
-        chunk(vcodes_hbm, values_ref, vsem, i).start()
-    for copy in small:
-        copy.wait()
+        chunk(vcodes_hbm, vbuf, vsem, i).start()
+    small[0].wait()
 
     lane = lax.broadcasted_iota(jnp.int32, (HEADS, LANES), 1)
     channels = chan_ref[...]
     for page in range(onehot.shape[0]):
         onehot[page] = (lane == channels[:, page : page + 1]).astype(F32)
-
+    none = jnp.zeros((HEADS, LANES), F32)
+    for copy in small[1:3]:
+        copy.wait()
+
+    @pl.loop(0, blocks)
+    def key_block(i):
+        chunk(kcodes_hbm, kbuf, ksem, i).wait()
+        first_page = i * PAGES
+        slots = [
+            outlier_ref[:, pl.ds(pl.multiple_of((first_page + p) * PAGE, PAGE), PAGE)].astype(F32)
+            for p in range(PAGES)
+        ]
+        slots = jnp.concatenate(slots + [none] * (LANES // HEADS - PAGES), axis=0).T.astype(BF16)
+        chosen = []
+        for p in range(PAGES):
+            column = [none] * (LANES // HEADS)
+            column[p] = onehot[first_page + p]
+            chosen.append(jnp.concatenate(column, axis=0).astype(BF16))
+        correction = jnp.dot(slots, jnp.concatenate(chosen, axis=1), preferred_element_type=F32)
+        for p in range(PAGES):
+            rows = pl.ds(pl.multiple_of((first_page + p) * PAGE, PAGE), PAGE)
+            base = kbuf[rows, :].astype(F32) * kscale_ref[first_page + p]
+            kbuf[rows, :] = (base + correction[:, p * LANES : (p + 1) * LANES]).astype(BF16)
+        pltpu.make_async_copy(
+            kbuf.at[block_rows(i), :], keys_hbm.at[block_rows(i), :], kout.at[i]
+        ).start()
+
+    for copy in small[3:]:
+        copy.wait()
     live = len_ref[0]
     own_scores = [
         jnp.where(
@@ -142,45 +180,36 @@
     own_ref[0] = jnp.broadcast_to(top, (HEADS, LANES))
     own_ref[1] = jnp.broadcast_to(jnp.sum(sums, axis=1, keepdims=True), (HEADS, LANES))
     own_ref[2] = weighted
-    none = jnp.zeros((HEADS, LANES), F32)
-
-    @pl.loop(0, blocks)
-    def key_block(i):
-        chunk(kcodes_hbm, keys_ref, ksem, i).wait()
-        first_page = i * PAGES
-        slots = [
-            outlier_ref[:, pl.ds(pl.multiple_of((first_page + p) * PAGE, PAGE), PAGE)].astype(F32)
-            for p in range(PAGES)
-        ]
-        slots = jnp.concatenate(slots + [none] * (LANES // HEADS - PAGES), axis=0).T.astype(BF16)
-        chosen = []
-        for p in range(PAGES):
-            column = [none] * (LANES // HEADS)
-            column[p] = onehot[first_page + p]
-            chosen.append(jnp.concatenate(column, axis=0).astype(BF16))
-        correction = jnp.dot(slots, jnp.concatenate(chosen, axis=1), preferred_element_type=F32)
-        for p in range(PAGES):
-            rows = pl.ds(pl.multiple_of((first_page + p) * PAGE, PAGE), PAGE)
-            base = keys_ref[rows, :].astype(F32) * kscale_ref[first_page + p]
-            keys_ref[rows, :] = (base + correction[:, p * LANES : (p + 1) * LANES]).astype(BF16)
+    result.start()
 
     @pl.loop(0, blocks)
     def value_block(i):
-        chunk(vcodes_hbm, values_ref, vsem, i).wait()
+        chunk(vcodes_hbm, vbuf, vsem, i).wait()
         for p in range(PAGES):
             rows = pl.ds(pl.multiple_of((i * PAGES + p) * PAGE, PAGE), PAGE)
-            values_ref[rows, :] = (
-                values_ref[rows, :].astype(F32) * vscale_ref[i * PAGES + p]
-            ).astype(BF16)
+            vbuf[rows, :] = (vbuf[rows, :].astype(F32) * vscale_ref[i * PAGES + p]).astype(BF16)
+        pltpu.make_async_copy(
+            vbuf.at[block_rows(i), :], values_hbm.at[block_rows(i), :], vout.at[i]
+        ).start()
+
+    for i in range(blocks):
+        pltpu.make_async_copy(
+            kbuf.at[block_rows(i), :], keys_hbm.at[block_rows(i), :], kout.at[i]
+        ).wait()
+        pltpu.make_async_copy(
+            vbuf.at[block_rows(i), :], values_hbm.at[block_rows(i), :], vout.at[i]
+        ).wait()
+    result.wait()
 
 
 def attend_kernel(
     place_ref,
     q_ref,
-    own_ref,
+    own_hbm,
     keys_hbm,
     values_hbm,
     out_ref,
+    own_ref,
     keys_ref,
     values_ref,
     scores,
@@ -190,7 +219,8 @@
     ksem,
     sem,
 ):
-    load = pltpu.make_async_copy(values_hbm, values_ref, sem)
+    load = pltpu.make_async_copy(values_hbm, values_ref, sem.at[0])
+    own_load = pltpu.make_async_copy(own_hbm.at[0], own_ref, sem.at[1])
 
     def chunk(i):
         rows = pl.ds(pl.multiple_of(i * BLOCK, BLOCK), BLOCK)
@@ -199,6 +229,7 @@
     for i in range(keys_ref.shape[0] // BLOCK):
         chunk(i).start()
     load.start()
+    own_load.start()
     blocks = keys_ref.shape[0] // BLOCK
     queries = q_ref.shape[0]
     peak[...] = jnp.full(peak.shape, LOW, F32)
@@ -220,8 +251,9 @@
     total[...] = jnp.zeros(total.shape, F32)
     acc[...] = jnp.zeros(acc.shape, F32)
     load.wait()
-
-    @pl.loop(0, blocks)
+    own_load.wait()
+
+    @pl.loop(0, blocks, unroll=True)
     def value_block(i):
         running = total[...]
         top = peak[...]
@@ -331,10 +363,10 @@
         out_shape=(
             jax.ShapeDtypeStruct((keys, LANES), BF16),
             jax.ShapeDtypeStruct((keys, LANES), BF16),
-            jax.ShapeDtypeStruct((3, HEADS, LANES), F32),
+            jax.ShapeDtypeStruct((ROOM, 3, HEADS, LANES), F32),
         ),
         in_specs=[HBM] * 11,
-        out_specs=(VMEM, VMEM, VMEM),
+        out_specs=(HBM, HBM, HBM),
         scratch_shapes=[
             pltpu.SMEM(suffix_len.shape, jnp.int32),
             pltpu.SMEM(page_table.shape, jnp.int32),
@@ -345,10 +377,15 @@
             pltpu.VMEM(value_scale.shape, F32),
             pltpu.VMEM((pools, PAGE, LANES), BF16),
             pltpu.VMEM((pools, PAGE, LANES), BF16),
+            pltpu.VMEM((keys, LANES), BF16),
+            pltpu.VMEM((keys, LANES), BF16),
+            pltpu.VMEM((3, HEADS, LANES), F32),
             pltpu.VMEM((keys // PAGE, HEADS, LANES), F32),
             pltpu.SemaphoreType.DMA((keys // BLOCK,)),
             pltpu.SemaphoreType.DMA((keys // BLOCK,)),
-            pltpu.SemaphoreType.DMA((9,)),
+            pltpu.SemaphoreType.DMA((keys // BLOCK,)),
+            pltpu.SemaphoreType.DMA((keys // BLOCK,)),
+            pltpu.SemaphoreType.DMA((10,)),
         ],
         compiler_params=pltpu.CompilerParams(vmem_limit_bytes=PREPARE_LIMIT),
         cost_estimate=pl.CostEstimate(
@@ -375,9 +412,10 @@
     return pl.pallas_call(
         attend_kernel,
         out_shape=jax.ShapeDtypeStruct((rows // SPLIT, SPLIT + STATS, LANES), BF16),
-        in_specs=[SMEM, VMEM, VMEM, HBM, HBM],
+        in_specs=[SMEM, VMEM, HBM, HBM, HBM],
         out_specs=VMEM,
         scratch_shapes=[
+            pltpu.VMEM(own.shape[1:], F32),
             pltpu.VMEM(keys.shape, BF16),
             pltpu.VMEM(values.shape, BF16),
             pltpu.VMEM((keys.shape[0] // TILE, rows, TILE), F32),
@@ -385,7 +423,7 @@
             pltpu.VMEM((rows, LANES), F32),
             pltpu.VMEM((rows, LANES), F32),
             pltpu.SemaphoreType.DMA((keys.shape[0] // BLOCK,)),
-            pltpu.SemaphoreType.DMA,
+            pltpu.SemaphoreType.DMA((2,)),
         ],
         compiler_params=pltpu.CompilerParams(vmem_limit_bytes=ATTEND_LIMIT),
         name="attend",

time: 102 us -> 98.4 us (0.965)
  Pallas kernels: 19.2 us -> 14.6 us
  waiting for transfers between devices: 6.62 us -> 8.35 us
    pallas_call x1, Pallas kernels: 10.5 us -> 7.62 us  [attend(): pl.pallas_call(attend_kernel, out_shape=jax.ShapeDtypeStruct((rows // SPL...]
    all_to_all x1, waiting for transfers between devices: 6.62 us -> 8.35 us  [spread(): return lax.all_to_all(copies, axis, 0, 0)]
    pallas_call x1, Pallas kernels: 7.62 us -> 5.89 us  [prepare(): pl.pallas_call(prepare_kernel, out_shape=(jax.ShapeDtypeStruct((keys, LAN...]
  transfers between devices with their start and end apart: 1 -> 1, of which waited for: 1 -> 1; matrix products, arithmetic and copies ran while one was open for 0% -> 0% of each run, Pallas kernels for 7% -> 6%
where the time goes in v5:
time: 98.4 us; the launch traced here: 98.1 us
  blocking collectives  53.8 us (55%)
  starting transfers between devices  19.3 us (20%)
  Pallas kernels  14.6 us (15%)
  waiting for transfers between devices  8.35 us (8%)
  local copies, waits for them, and re-layouts  1.35 us (1%)
    all_to_all x1, starting transfers between devices, spread(): return lax.all_to_all(copies, axis, 0, 0)  19.3 us
    all_to_all x1, blocking collectives, shards(): partial = lax.all_to_all(partial, far, 0, 0)  16.3 us
    all_to_all x1, blocking collectives, shards(): lax.all_to_all(product.reshape(tp, samples // tp, LANES), ('x', 'core'),...  14.4 us
    all_to_all x1, blocking collectives, shards(): partial = lax.all_to_all(partial, near, 0, 0)  12.5 us
    all_to_all x1, blocking collectives, shards(): attention = lax.all_to_all(attention, near, 0, 0)  10.5 us
    all_to_all x1, waiting for transfers between devices, spread(): return lax.all_to_all(copies, axis, 0, 0)  8.35 us
    pallas_call x1, Pallas kernels, attend(): pl.pallas_call(attend_kernel, out_shape=jax.ShapeDtypeStruct((rows // SPL...  7.62 us
    pallas_call x1, Pallas kernels, prepare(): pl.pallas_call(prepare_kernel, out_shape=(jax.ShapeDtypeStruct((keys, LAN...  5.89 us
  transfers between devices with their start and end apart: 1, of which 1 were waited for; matrix products, arithmetic and copies ran while one was open for 0% of the time, Pallas kernels for 6%

profile of v5, /device:TPU:1, one launch (start us, length us, event | category | flops | bytes accessed | tf_op | source)
XLA Modules:
  0.0 98.1 jit_solution(9780404421214967093)
XLA Ops:
  0.0 1.3 %broadcast_in_dim.8 = bf16[64,8,128]{2,1,0:T(8,128)(2,1)} broadcast(bf16[8,128]{1,0:T(8,128)(2,1)} %bitcast.21), dimensions={1,2} | broadcast | bytes 133120 | tf_op jit(solution)/shard_map/broadcast_in_dim | solution.py:342
  1.3 19.3 %all-to-all-start = ((bf16[64,8,128]{2,1,0:T(8,128)(2,1)}), bf16[64,8,128]{2,1,0:T(8,128)(2,1)S(1)}, u32[]{:S(2)}, u32[]{:S(2)}) async-start(bf16[64,8,128]{2,1,0:T(8,128)(2,1)} %broadcast_in_dim.8), calls=%async_computation | async-start | bytes 262144 | tf_op jit(solution)/shard_map/all_to_all | solution.py:343
  21.3 5.9 %prepare.1 = (bf16[8192,128]{1,0:T(8,128)(2,1)}, bf16[8192,128]{1,0:T(8,128)(2,1)}, f32[256,3,8,128]{3,2,1,0:T(8,128)}) custom-call(s32[1]{0:T(128)S(6)} %copy.13.len_hbm, s32[1,4]{1,0:T(1,128)} %table_hbm.1, bf16[8,128]{1,0:T(8,128)(2,1)} %bitcast.22, f32[64,1,128]{2,1,0:T(1,128)} %kscale_hbm.1, s32[8,64]{1,0:T(8,128)} %bitcast.23, ...), custom_call_target="tpu_custom_call" | custom-call | flops 268435456 | bytes 10485760 | tf_op jit(solution)/shard_map/prepare/pallas_call | solution.py:361
  27.2 8.4 %all-to-all-done = bf16[64,8,128]{2,1,0:T(8,128)(2,1)S(1)} async-done(((bf16[64,8,128]{2,1,0:T(8,128)(2,1)}), bf16[64,8,128]{2,1,0:T(8,128)(2,1)S(1)}, u32[]{:S(2)}, u32[]{:S(2)}) %all-to-all-start) | async-done | bytes 131104 | tf_op jit(solution)/shard_map/all_to_all | solution.py:343
  35.5 0.0 copy-start
  35.5 7.6 %attend.1 = bf16[16,48,128]{2,1,0:T(8,128)(2,1)S(1)} custom-call(s32[1]{0:T(128)} %bitcast.place_ref, bf16[512,128]{1,0:T(8,128)(2,1)S(1)} %bitcast.14, f32[256,3,8,128]{3,2,1,0:T(8,128)} %get-tuple-element.8.own_hbm, bf16[8192,128]{1,0:T(8,128)(2,1)} %get-tuple-element.9.keys_hbm, bf16[8192,128]{1,0:T(8,128)(2,1)} %get-tuple-element.10.values_hbm), custom_call_target="tpu_custom_call" | custom-call | tf_op jit(solution)/shard_map/attend/pallas_call | solution.py:412
  43.2 12.5 %all_to_all.25.in_ref = bf16[16,48,128]{2,1,0:T(8,128)(2,1)S(1)} all-to-all(bf16[16,48,128]{2,1,0:T(8,128)(2,1)S(1)} %attend.1), channel_id=1, replica_groups=mesh['zh'=4,'zl'=4,'y'=4,'x'=4,'core'=2] {'zl','y'}, dimensions={0} | all-to-all | bytes 393216 | tf_op jit(solution)/shard_map/all_to_all | solution.py:467
  55.7 0.2 merge_near.1
  55.9 16.3 %all_to_all.26.in_ref = bf16[4,48,128]{2,1,0:T(8,128)(2,1)S(1)} all-to-all(bf16[4,48,128]{2,1,0:T(8,128)(2,1)S(1)} %merge_near.1), channel_id=1, replica_groups=mesh['zh'=4,'zl'=4,'y'=4,'x'=4,'core'=2] {'zh'}, dimensions={0} | all-to-all | bytes 98304 | tf_op jit(solution)/shard_map/all_to_all | solution.py:476
  72.2 0.1 merge_far.1
  72.3 10.5 %all_to_all.27.in_ref = bf16[16,32,128]{2,1,0:T(8,128)(2,1)S(1)} all-to-all(bf16[16,32,128]{2,1,0:T(8,128)(2,1)S(1)} %merge_far.1), channel_id=1, replica_groups=mesh['zh'=4,'zl'=4,'y'=4,'x'=4,'core'=2] {'zl','y'}, dimensions={0} | all-to-all | bytes 262144 | tf_op jit(solution)/shard_map/all_to_all | solution.py:485
  82.8 0.0 copy-done
  82.8 0.2 project.1
  83.0 14.4 %all_to_all.28.in_ref = bf16[8,8,128]{2,1,0:T(8,128)(2,1)S(1)} all-to-all(bf16[8,8,128]{2,1,0:T(8,128)(2,1)S(1)} %bitcast.15), channel_id=1, replica_groups=mesh['zh'=4,'zl'=4,'y'=4,'x'=4,'core'=2] {'x','core'}, dimensions={0} | all-to-all | bytes 32768 | tf_op jit(solution)/shard_map/all_to_all | solution.py:496
  97.5 0.6 sum_tp.1
Async XLA Ops:
  1.3 34.2 %all-to-all-start = ((bf16[64,8,128]{2,1,0:T(8,128)(2,1)}), bf16[64,8,128]{2,1,0:T(8,128)(2,1)S(1)}, u32[]{:S(2)}, u32[]{:S(2)}) async-start(bf16[64,8,128]{2,1,0:T(8,128)(2,1)} %broadcast_in_dim.8), calls=%async_computation | async-start | bytes 262144 | tf_op jit(solution)/shard_map/all_to_all | solution.py:343
  35.5 47.3 %copy-start = (bf16[1024,128]{1,0:T(8,128)(2,1)S(1)}, bf16[1024,128]{1,0:T(8,128)(2,1)}, u32[]{:S(2)}) copy-start(bf16[1024,128]{1,0:T(8,128)(2,1)} %weight_ref.1) | copy-start | bytes 786436

commit v6 on v5

--- a/solution.py
+++ b/solution.py
@@ -19,6 +19,7 @@
 PAGES = BLOCK // PAGE
 SCORE_SCALE = math.log2(math.e) / math.sqrt(LANES)
 SPLIT = 32
+GROUP = 64
 STATS = 16
 LOW = -1e30
 VMEM = pl.BlockSpec(memory_space=pltpu.VMEM)
@@ -47,6 +48,15 @@
     row = lax.broadcasted_iota(jnp.int32, columns.shape, 0)
     lane = lax.broadcasted_iota(jnp.int32, columns.shape, 1)
     return jnp.sum(jnp.where(lane % SPLIT == row, columns, 0.0), axis=0, keepdims=True)
+
+
+def stat_rows(logs):
+    copies = STATS * SPLIT // GROUP
+    rows = [
+        jnp.broadcast_to(to_lanes(logs[at : at + SPLIT]), (copies, LANES))
+        for at in range(0, GROUP, SPLIT)
+    ]
+    return split_rows(jnp.concatenate(rows, axis=0))
 
 
 def to_rows(stat):
@@ -280,48 +290,49 @@
     acc[own, :] = acc[own, :] * fade + own_ref[2] * own_fade
 
     pieces = out_ref.shape[0]
-    stride = queries // SPLIT * HEADS
     for c in range(pieces):
         rows = [
-            slice(u * stride + c * HEADS, u * stride + (c + 1) * HEADS)
-            for u in range(SPLIT // HEADS)
+            slice((u * pieces + c) * HEADS, (u * pieces + c + 1) * HEADS)
+            for u in range(GROUP // HEADS)
         ]
         part = [acc[r, :] / total[r, :] for r in rows]
         logs = [peak[r, :] + jnp.log2(total[r, :]) for r in rows]
-        out_ref[c, :SPLIT, :] = jnp.concatenate(part, axis=0).astype(BF16)
-        stat = split_rows(to_lanes(jnp.concatenate(logs, axis=0)))
-        out_ref[c, SPLIT:, :] = jnp.broadcast_to(stat, (STATS, LANES))
+        out_ref[c, :GROUP, :] = jnp.concatenate(part, axis=0).astype(BF16)
+        out_ref[c, GROUP:, :] = stat_rows(jnp.concatenate(logs, axis=0))
 
 
 def merge_kernel(in_ref, out_ref):
     sources = in_ref.shape[0]
-    logs = [to_rows(in_ref[s, SPLIT:, :].astype(F32)[:1]) for s in range(sources)]
+    logs = []
+    for s in range(sources):
+        stats = in_ref[s, GROUP:, :].astype(F32)
+        first = [at * STATS // GROUP for at in range(0, GROUP, SPLIT)]
+        logs.append(jnp.concatenate([to_rows(stats[at : at + 1]) for at in first], axis=0))
     top = functools.reduce(jnp.maximum, logs)
     sums = jnp.zeros(top.shape, F32)
-    weighted = jnp.zeros((SPLIT, LANES), F32)
+    weighted = jnp.zeros((GROUP, LANES), F32)
     for s in range(sources):
         weight = jnp.exp2(logs[s] - top)
         sums = sums + weight
-        weighted = weighted + in_ref[s, :SPLIT, :].astype(F32) * weight
+        weighted = weighted + in_ref[s, :GROUP, :].astype(F32) * weight
     merged = (weighted / sums).astype(BF16)
     copies, rows, lanes = out_ref.shape
-    if rows > SPLIT:
-        wide = jnp.broadcast_to(top + jnp.log2(sums), (SPLIT, LANES))
-        stat = jnp.broadcast_to(split_rows(to_lanes(wide)), (STATS, LANES))
+    if rows > GROUP:
+        stat = stat_rows(jnp.broadcast_to(top + jnp.log2(sums), (GROUP, LANES)))
     for c in range(copies):
-        out_ref[c, :SPLIT, :] = merged
-        if rows > SPLIT:
-            out_ref[c, SPLIT:, :] = stat
+        out_ref[c, :GROUP, :] = merged
+        if rows > GROUP:
+            out_ref[c, GROUP:, :] = stat
 
 
 def project_kernel(in_ref, weight_ref, out_ref, wide):
     blocks = in_ref.shape[0]
     for c in range(blocks):
         block = in_ref[c].astype(F32)
-        for u in range(SPLIT // HEADS):
+        for u in range(GROUP // HEADS):
             first = (u * blocks + c) * HEADS
             wide[first : first + HEADS, :] = block[u * HEADS : (u + 1) * HEADS]
-    samples = blocks * SPLIT // HEADS
+    samples = blocks * GROUP // HEADS
     result = jnp.zeros((samples, LANES), F32)
     for h in range(HEADS):
         part = wide[pl.ds(h, samples, stride=HEADS), :].astype(BF16)
@@ -411,7 +422,7 @@
     rows = all_queries.shape[0]
     return pl.pallas_call(
         attend_kernel,
-        out_shape=jax.ShapeDtypeStruct((rows // SPLIT, SPLIT + STATS, LANES), BF16),
+        out_shape=jax.ShapeDtypeStruct((rows // GROUP, GROUP + STATS, LANES), BF16),
         in_specs=[SMEM, VMEM, HBM, HBM, HBM],
         out_specs=VMEM,
         scratch_shapes=[
@@ -467,7 +478,7 @@
     partial = lax.all_to_all(partial, near, 0, 0)
     partial = pl.pallas_call(
         merge_kernel,
-        out_shape=jax.ShapeDtypeStruct((lax.axis_size(far), SPLIT + STATS, LANES), BF16),
+        out_shape=jax.ShapeDtypeStruct((lax.axis_size(far), GROUP + STATS, LANES), BF16),
         in_specs=[VMEM],
         out_specs=VMEM,
         compiler_params=params,
@@ -476,7 +487,7 @@
     partial = lax.all_to_all(partial, far, 0, 0)
     attention = pl.pallas_call(
         merge_kernel,
-        out_shape=jax.ShapeDtypeStruct((lax.axis_size(near), SPLIT, LANES), BF16),
+        out_shape=jax.ShapeDtypeStruct((lax.axis_size(near), GROUP, LANES), BF16),
         in_specs=[VMEM],
         out_specs=VMEM,
         compiler_params=params,
@@ -505,7 +516,7 @@
 
 
 def solution(mesh):
-    grid = Mesh(mesh.devices.reshape(4, 4, 4, 4, 2), ("zh", "zl", "y", "x", "core"))
+    grid = Mesh(mesh.devices.reshape(8, 2, 4, 4, 2), ("zh", "zl", "y", "x", "core"))
     seq, tp = ("zh", "zl", "y"), ("x", "core")
     return jax.shard_map(
         shards,

time: 98.4 us -> 93.8 us (0.953)
  blocking collectives: 53.8 us -> 48.8 us
    all_to_all x1, blocking collectives: 12.5 us -> 9.24 us  [shards(): partial = lax.all_to_all(partial, near, 0, 0)]
    all_to_all x1, blocking collectives: 10.5 us -> 7.82 us  [shards(): attention = lax.all_to_all(attention, near, 0, 0)]
    all_to_all x1, blocking collectives: 16.3 us -> 17.5 us  [shards(): partial = lax.all_to_all(partial, far, 0, 0)]
where the time goes in v6:
time: 93.8 us; the launch traced here: 93.4 us
  blocking collectives  48.8 us (52%)
  starting transfers between devices  19.3 us (21%)
  Pallas kernels  15 us (16%)
  waiting for transfers between devices  8.35 us (9%)
  local copies, waits for them, and re-layouts  1.35 us (1%)
    all_to_all x1, starting transfers between devices, spread(): return lax.all_to_all(copies, axis, 0, 0)  19.3 us
    all_to_all x1, blocking collectives, shards(): partial = lax.all_to_all(partial, far, 0, 0)  17.5 us
    all_to_all x1, blocking collectives, shards(): lax.all_to_all(product.reshape(tp, samples // tp, LANES), ('x', 'core'),...  14.2 us
    all_to_all x1, blocking collectives, shards(): partial = lax.all_to_all(partial, near, 0, 0)  9.24 us
    all_to_all x1, waiting for transfers between devices, spread(): return lax.all_to_all(copies, axis, 0, 0)  8.35 us
    all_to_all x1, blocking collectives, shards(): attention = lax.all_to_all(attention, near, 0, 0)  7.82 us
    pallas_call x1, Pallas kernels, attend(): pl.pallas_call(attend_kernel, out_shape=jax.ShapeDtypeStruct((rows // GRO...  7.63 us
    pallas_call x1, Pallas kernels, prepare(): pl.pallas_call(prepare_kernel, out_shape=(jax.ShapeDtypeStruct((keys, LAN...  5.89 us
  transfers between devices with their start and end apart: 1, of which 1 were waited for; matrix products, arithmetic and copies ran while one was open for 0% of the time, Pallas kernels for 6%

profile of v6, /device:TPU:1, one launch (start us, length us, event | category | flops | bytes accessed | tf_op | source)
XLA Modules:
  0.0 93.4 jit_solution(18222364533149991269)
XLA Ops:
  0.0 1.3 %broadcast_in_dim.8 = bf16[64,8,128]{2,1,0:T(8,128)(2,1)} broadcast(bf16[8,128]{1,0:T(8,128)(2,1)} %bitcast.21), dimensions={1,2} | broadcast | bytes 133120 | tf_op jit(solution)/shard_map/broadcast_in_dim | solution.py:353
  1.3 19.3 %all-to-all-start = ((bf16[64,8,128]{2,1,0:T(8,128)(2,1)}), bf16[64,8,128]{2,1,0:T(8,128)(2,1)S(1)}, u32[]{:S(2)}, u32[]{:S(2)}) async-start(bf16[64,8,128]{2,1,0:T(8,128)(2,1)} %broadcast_in_dim.8), calls=%async_computation | async-start | bytes 262144 | tf_op jit(solution)/shard_map/all_to_all | solution.py:354
  21.3 5.9 %prepare.1 = (bf16[8192,128]{1,0:T(8,128)(2,1)}, bf16[8192,128]{1,0:T(8,128)(2,1)}, f32[256,3,8,128]{3,2,1,0:T(8,128)}) custom-call(s32[1]{0:T(128)S(6)} %copy.13.len_hbm, s32[1,4]{1,0:T(1,128)} %table_hbm.1, bf16[8,128]{1,0:T(8,128)(2,1)} %bitcast.22, f32[64,1,128]{2,1,0:T(1,128)} %kscale_hbm.1, s32[8,64]{1,0:T(8,128)} %bitcast.23, ...), custom_call_target="tpu_custom_call" | custom-call | flops 268435456 | bytes 10485760 | tf_op jit(solution)/shard_map/prepare/pallas_call | solution.py:372
  27.2 8.4 %all-to-all-done = bf16[64,8,128]{2,1,0:T(8,128)(2,1)S(1)} async-done(((bf16[64,8,128]{2,1,0:T(8,128)(2,1)}), bf16[64,8,128]{2,1,0:T(8,128)(2,1)S(1)}, u32[]{:S(2)}, u32[]{:S(2)}) %all-to-all-start) | async-done | bytes 131104 | tf_op jit(solution)/shard_map/all_to_all | solution.py:354
  35.5 0.0 copy-start
  35.5 7.6 %attend.1 = bf16[8,80,128]{2,1,0:T(8,128)(2,1)S(1)} custom-call(s32[1]{0:T(128)} %bitcast.place_ref, bf16[512,128]{1,0:T(8,128)(2,1)S(1)} %bitcast.14, f32[256,3,8,128]{3,2,1,0:T(8,128)} %get-tuple-element.8.own_hbm, bf16[8192,128]{1,0:T(8,128)(2,1)} %get-tuple-element.9.keys_hbm, bf16[8192,128]{1,0:T(8,128)(2,1)} %get-tuple-element.10.values_hbm), custom_call_target="tpu_custom_call" | custom-call | tf_op jit(solution)/shard_map/attend/pallas_call | solution.py:423
  43.2 9.2 %all_to_all.25.in_ref = bf16[8,80,128]{2,1,0:T(8,128)(2,1)S(1)} all-to-all(bf16[8,80,128]{2,1,0:T(8,128)(2,1)S(1)} %attend.1), channel_id=1, replica_groups=mesh['zh'=8,'zl'=2,'y'=4,'x'=4,'core'=2] {'zl','y'}, dimensions={0} | all-to-all | bytes 327680 | tf_op jit(solution)/shard_map/all_to_all | solution.py:478
  52.4 0.4 merge_near.1
  52.8 17.5 %all_to_all.26.in_ref = bf16[8,80,128]{2,1,0:T(8,128)(2,1)S(1)} all-to-all(bf16[8,80,128]{2,1,0:T(8,128)(2,1)S(1)} %merge_near.1), channel_id=1, replica_groups=mesh['zh'=8,'zl'=2,'y'=4,'x'=4,'core'=2] {'zh'}, dimensions={0} | all-to-all | bytes 327680 | tf_op jit(solution)/shard_map/all_to_all | solution.py:487
  70.3 0.3 merge_far.1
  70.6 7.8 %all_to_all.27.in_ref = bf16[8,64,128]{2,1,0:T(8,128)(2,1)S(1)} all-to-all(bf16[8,64,128]{2,1,0:T(8,128)(2,1)S(1)} %merge_far.1), channel_id=1, replica_groups=mesh['zh'=8,'zl'=2,'y'=4,'x'=4,'core'=2] {'zl','y'}, dimensions={0} | all-to-all | bytes 262144 | tf_op jit(solution)/shard_map/all_to_all | solution.py:496
  78.4 0.0 copy-done
  78.4 0.2 project.1
  78.6 14.2 %all_to_all.28.in_ref = bf16[8,8,128]{2,1,0:T(8,128)(2,1)S(1)} all-to-all(bf16[8,8,128]{2,1,0:T(8,128)(2,1)S(1)} %bitcast.15), channel_id=1, replica_groups=mesh['zh'=8,'zl'=2,'y'=4,'x'=4,'core'=2] {'x','core'}, dimensions={0} | all-to-all | bytes 32768 | tf_op jit(solution)/shard_map/all_to_all | solution.py:507
  92.8 0.6 sum_tp.1
Async XLA Ops:
  1.3 34.2 %all-to-all-start = ((bf16[64,8,128]{2,1,0:T(8,128)(2,1)}), bf16[64,8,128]{2,1,0:T(8,128)(2,1)S(1)}, u32[]{:S(2)}, u32[]{:S(2)}) async-start(bf16[64,8,128]{2,1,0:T(8,128)(2,1)} %broadcast_in_dim.8), calls=%async_computation | async-start | bytes 262144 | tf_op jit(solution)/shard_map/all_to_all | solution.py:354
  35.5 42.9 %copy-start = (bf16[1024,128]{1,0:T(8,128)(2,1)S(1)}, bf16[1024,128]{1,0:T(8,128)(2,1)}, u32[]{:S(2)}) copy-start(bf16[1024,128]{1,0:T(8,128)(2,1)} %weight_ref.1) | copy-start | bytes 786436

commit v7 on v6

--- a/solution.py
+++ b/solution.py
@@ -458,7 +458,7 @@
     seq, near, far = ("zh", "zl", "y"), ("zl", "y"), "zh"
     samples = lax.axis_size(seq)
     queries = queries.reshape(HEADS, LANES)
-    all_queries = spread(queries, seq).reshape(samples * HEADS, LANES)
+    all_queries = spread(spread(queries, near), far).reshape(samples * HEADS, LANES)
     own = lax.axis_index(seq).astype(jnp.int32).reshape(1)
     params = pltpu.CompilerParams(vmem_limit_bytes=SMALL)
     prepared = prepare(

time: 93.8 us -> 98.7 us (1.052)
  blocking collectives: 48.8 us -> 60.7 us
  starting transfers between devices: 19.3 us -> 13.9 us
  waiting for transfers between devices: 8.35 us -> 6.64 us
    all_to_all x0 -> x1, blocking collectives: none -> 11.2 us  [spread(): return lax.all_to_all(copies, axis, 0, 0)]
    all_to_all x1, starting transfers between devices: 19.3 us -> 13.9 us  [spread(): return lax.all_to_all(copies, axis, 0, 0)]
    all_to_all x1, waiting for transfers between devices: 8.35 us -> 6.64 us  [spread(): return lax.all_to_all(copies, axis, 0, 0)]
    all_to_all x1, blocking collectives: 9.24 us -> 8.01 us  [shards(): partial = lax.all_to_all(partial, near, 0, 0)]
    all_to_all x1, blocking collectives: 14.2 us -> 15.3 us  [shards(): lax.all_to_all(product.reshape(tp, samples // tp, LANES), ('x', 'core'),...]
where the time goes in v7:
time: 98.7 us; the launch traced here: 98.3 us
  blocking collectives  60.7 us (61%)
  Pallas kernels  15 us (15%)
  starting transfers between devices  13.9 us (14%)
  waiting for transfers between devices  6.64 us (7%)
  local copies, waits for them, and re-layouts  1.35 us (1%)
    all_to_all x1, blocking collectives, shards(): partial = lax.all_to_all(partial, far, 0, 0)  18.4 us
    all_to_all x1, blocking collectives, shards(): lax.all_to_all(product.reshape(tp, samples // tp, LANES), ('x', 'core'),...  15.3 us
    all_to_all x1, starting transfers between devices, spread(): return lax.all_to_all(copies, axis, 0, 0)  13.9 us
    all_to_all x1, blocking collectives, spread(): return lax.all_to_all(copies, axis, 0, 0)  11.2 us
    all_to_all x1, blocking collectives, shards(): partial = lax.all_to_all(partial, near, 0, 0)  8.01 us
    all_to_all x1, blocking collectives, shards(): attention = lax.all_to_all(attention, near, 0, 0)  7.82 us
    pallas_call x1, Pallas kernels, attend(): pl.pallas_call(attend_kernel, out_shape=jax.ShapeDtypeStruct((rows // GRO...  7.62 us
    all_to_all x1, waiting for transfers between devices, spread(): return lax.all_to_all(copies, axis, 0, 0)  6.64 us
  transfers between devices with their start and end apart: 1, of which 1 were waited for; matrix products, arithmetic and copies ran while one was open for 0% of the time, Pallas kernels for 6%

profile of v7, /device:TPU:1, one launch (start us, length us, event | category | flops | bytes accessed | tf_op | source)
XLA Modules:
  0.0 98.3 jit_solution(12853160519660198852)
XLA Ops:
  0.0 0.7 broadcast_in_dim.14
  0.7 11.2 %all_to_all.30 = bf16[8,8,128]{2,1,0:T(8,128)(2,1)S(1)} all-to-all(bf16[8,8,128]{2,1,0:T(8,128)(2,1)S(1)} %broadcast_in_dim.14), channel_id=1, replica_groups=mesh['zh'=8,'zl'=2,'y'=4,'x'=4,'core'=2] {'zl','y'}, dimensions={0} | all-to-all | bytes 32768 | tf_op jit(solution)/shard_map/all_to_all | solution.py:354
  11.9 0.7 broadcast_in_dim.15
  12.6 13.9 %all-to-all-start.1 = ((bf16[8,8,8,128]{3,2,1,0:T(8,128)(2,1)}), bf16[8,8,8,128]{3,2,1,0:T(8,128)(2,1)S(1)}, u32[]{:S(2)}, u32[]{:S(2)}) async-start(bf16[8,8,8,128]{3,2,1,0:T(8,128)(2,1)} %broadcast_in_dim.15), calls=%async_computation.1 | async-start | bytes 262144 | tf_op jit(solution)/shard_map/all_to_all | solution.py:354
  27.1 5.9 %prepare.1 = (bf16[8192,128]{1,0:T(8,128)(2,1)}, bf16[8192,128]{1,0:T(8,128)(2,1)}, f32[256,3,8,128]{3,2,1,0:T(8,128)}) custom-call(s32[1]{0:T(128)S(6)} %copy.13.len_hbm, s32[1,4]{1,0:T(1,128)} %table_hbm.1, bf16[8,128]{1,0:T(8,128)(2,1)} %bitcast.22, f32[64,1,128]{2,1,0:T(1,128)} %kscale_hbm.1, s32[8,64]{1,0:T(8,128)} %bitcast.23, ...), custom_call_target="tpu_custom_call" | custom-call | flops 268435456 | bytes 10485760 | tf_op jit(solution)/shard_map/prepare/pallas_call | solution.py:372
  33.0 6.6 %all-to-all-done.1 = bf16[8,8,8,128]{3,2,1,0:T(8,128)(2,1)S(1)} async-done(((bf16[8,8,8,128]{3,2,1,0:T(8,128)(2,1)}), bf16[8,8,8,128]{3,2,1,0:T(8,128)(2,1)S(1)}, u32[]{:S(2)}, u32[]{:S(2)}) %all-to-all-start.1) | async-done | bytes 131104 | tf_op jit(solution)/shard_map/all_to_all | solution.py:354
  39.7 0.0 copy-start
  39.7 7.6 %attend.1 = bf16[8,80,128]{2,1,0:T(8,128)(2,1)S(1)} custom-call(s32[1]{0:T(128)} %bitcast.place_ref, bf16[512,128]{1,0:T(8,128)(2,1)S(1)} %bitcast.14, f32[256,3,8,128]{3,2,1,0:T(8,128)} %get-tuple-element.8.own_hbm, bf16[8192,128]{1,0:T(8,128)(2,1)} %get-tuple-element.9.keys_hbm, bf16[8192,128]{1,0:T(8,128)(2,1)} %get-tuple-element.10.values_hbm), custom_call_target="tpu_custom_call" | custom-call | tf_op jit(solution)/shard_map/attend/pallas_call | solution.py:423
  47.3 8.0 %all_to_all.31.in_ref = bf16[8,80,128]{2,1,0:T(8,128)(2,1)S(1)} all-to-all(bf16[8,80,128]{2,1,0:T(8,128)(2,1)S(1)} %attend.1), channel_id=1, replica_groups=mesh['zh'=8,'zl'=2,'y'=4,'x'=4,'core'=2] {'zl','y'}, dimensions={0} | all-to-all | bytes 327680 | tf_op jit(solution)/shard_map/all_to_all | solution.py:478
  55.3 0.4 merge_near.1
  55.7 18.4 %all_to_all.32.in_ref = bf16[8,80,128]{2,1,0:T(8,128)(2,1)S(1)} all-to-all(bf16[8,80,128]{2,1,0:T(8,128)(2,1)S(1)} %merge_near.1), channel_id=1, replica_groups=mesh['zh'=8,'zl'=2,'y'=4,'x'=4,'core'=2] {'zh'}, dimensions={0} | all-to-all | bytes 327680 | tf_op jit(solution)/shard_map/all_to_all | solution.py:487
  74.1 0.3 merge_far.1
  74.4 7.8 %all_to_all.33.in_ref = bf16[8,64,128]{2,1,0:T(8,128)(2,1)S(1)} all-to-all(bf16[8,64,128]{2,1,0:T(8,128)(2,1)S(1)} %merge_far.1), channel_id=1, replica_groups=mesh['zh'=8,'zl'=2,'y'=4,'x'=4,'core'=2] {'zl','y'}, dimensions={0} | all-to-all | bytes 262144 | tf_op jit(solution)/shard_map/all_to_all | solution.py:496
  82.2 0.0 copy-done
  82.2 0.2 project.1
  82.4 15.3 %all_to_all.34.in_ref = bf16[8,8,128]{2,1,0:T(8,128)(2,1)S(1)} all-to-all(bf16[8,8,128]{2,1,0:T(8,128)(2,1)S(1)} %bitcast.15), channel_id=1, replica_groups=mesh['zh'=8,'zl'=2,'y'=4,'x'=4,'core'=2] {'x','core'}, dimensions={0} | all-to-all | bytes 32768 | tf_op jit(solution)/shard_map/all_to_all | solution.py:507
  97.7 0.6 sum_tp.1
Async XLA Ops:
  12.6 27.1 %all-to-all-start.1 = ((bf16[8,8,8,128]{3,2,1,0:T(8,128)(2,1)}), bf16[8,8,8,128]{3,2,1,0:T(8,128)(2,1)S(1)}, u32[]{:S(2)}, u32[]{:S(2)}) async-start(bf16[8,8,8,128]{3,2,1,0:T(8,128)(2,1)} %broadcast_in_dim.15), calls=%async_computation.1 | async-start | bytes 262144 | tf_op jit(solution)/shard_map/all_to_all | solution.py:354
  39.7 42.6 %copy-start = (bf16[1024,128]{1,0:T(8,128)(2,1)S(1)}, bf16[1024,128]{1,0:T(8,128)(2,1)}, u32[]{:S(2)}) copy-start(bf16[1024,128]{1,0:T(8,128)(2,1)} %weight_ref.1) | copy-start | bytes 786436

commit v8 on v6

--- a/solution.py
+++ b/solution.py
@@ -14,13 +14,14 @@
 HEADS = 8
 PAGE = 128
 TILE = 256
-BLOCK = 1024
+BLOCK = 2048
+WEIGHT_STEP = 1024
 ROOM = 256
 PAGES = BLOCK // PAGE
 SCORE_SCALE = math.log2(math.e) / math.sqrt(LANES)
 SPLIT = 32
 GROUP = 64
-STATS = 16
+STATS = 8
 LOW = -1e30
 VMEM = pl.BlockSpec(memory_space=pltpu.VMEM)
 SMEM = pl.BlockSpec(memory_space=pltpu.SMEM)
@@ -263,19 +264,19 @@
     load.wait()
     own_load.wait()
 
-    @pl.loop(0, blocks, unroll=True)
+    @pl.loop(0, keys_ref.shape[0] // WEIGHT_STEP, unroll=True)
     def value_block(i):
         running = total[...]
         top = peak[...]
         weights = []
-        for j in range(BLOCK // TILE):
+        for j in range(WEIGHT_STEP // TILE):
             for p in range(TILE // PAGE):
-                part = scores[i * (BLOCK // TILE) + j, :, p * LANES : (p + 1) * LANES]
+                part = scores[i * (WEIGHT_STEP // TILE) + j, :, p * LANES : (p + 1) * LANES]
                 weight = jnp.exp2(part * SCORE_SCALE - top)
                 running = running + weight
                 weights.append(weight.astype(BF16))
         total[...] = running
-        rows = pl.ds(pl.multiple_of(i * BLOCK, BLOCK), BLOCK)
+        rows = pl.ds(pl.multiple_of(i * WEIGHT_STEP, WEIGHT_STEP), WEIGHT_STEP)
         acc[...] += jnp.dot(
             jnp.concatenate(weights, axis=1), values_ref[rows, :], preferred_element_type=F32
         )

time: 93.8 us -> 92.6 us (0.987)
  Pallas kernels: 15 us -> 13.5 us
where the time goes in v8:
time: 92.6 us; the launch traced here: 92.2 us
  blocking collectives  48.2 us (52%)
  starting transfers between devices  19.3 us (21%)
  Pallas kernels  13.5 us (15%)
  waiting for transfers between devices  9.17 us (10%)
  local copies, waits for them, and re-layouts  1.35 us (1%)
    all_to_all x1, starting transfers between devices, spread(): return lax.all_to_all(copies, axis, 0, 0)  19.3 us
    all_to_all x1, blocking collectives, shards(): partial = lax.all_to_all(partial, far, 0, 0)  17.4 us
    all_to_all x1, blocking collectives, shards(): lax.all_to_all(product.reshape(tp, samples // tp, LANES), ('x', 'core'),...  13.8 us
    all_to_all x1, waiting for transfers between devices, spread(): return lax.all_to_all(copies, axis, 0, 0)  9.17 us
    all_to_all x1, blocking collectives, shards(): partial = lax.all_to_all(partial, near, 0, 0)  9.16 us
    all_to_all x1, blocking collectives, shards(): attention = lax.all_to_all(attention, near, 0, 0)  7.82 us
    pallas_call x1, Pallas kernels, attend(): pl.pallas_call(attend_kernel, out_shape=jax.ShapeDtypeStruct((rows // GRO...  7 us
    pallas_call x1, Pallas kernels, prepare(): pl.pallas_call(prepare_kernel, out_shape=(jax.ShapeDtypeStruct((keys, LAN...  5.07 us
  transfers between devices with their start and end apart: 1, of which 1 were waited for; matrix products, arithmetic and copies ran while one was open for 0% of the time, Pallas kernels for 6%

profile of v8, /device:TPU:1, one launch (start us, length us, event | category | flops | bytes accessed | tf_op | source)
XLA Modules:
  0.0 92.2 jit_solution(12235750882808396287)
XLA Ops:
  0.0 1.3 %broadcast_in_dim.8 = bf16[64,8,128]{2,1,0:T(8,128)(2,1)} broadcast(bf16[8,128]{1,0:T(8,128)(2,1)} %bitcast.21), dimensions={1,2} | broadcast | bytes 133120 | tf_op jit(solution)/shard_map/broadcast_in_dim | solution.py:354
  1.3 19.3 %all-to-all-start = ((bf16[64,8,128]{2,1,0:T(8,128)(2,1)}), bf16[64,8,128]{2,1,0:T(8,128)(2,1)S(1)}, u32[]{:S(2)}, u32[]{:S(2)}) async-start(bf16[64,8,128]{2,1,0:T(8,128)(2,1)} %broadcast_in_dim.8), calls=%async_computation | async-start | bytes 262144 | tf_op jit(solution)/shard_map/all_to_all | solution.py:355
  21.3 5.1 %prepare.1 = (bf16[8192,128]{1,0:T(8,128)(2,1)}, bf16[8192,128]{1,0:T(8,128)(2,1)}, f32[256,3,8,128]{3,2,1,0:T(8,128)}) custom-call(s32[1]{0:T(128)S(6)} %copy.13.len_hbm, s32[1,4]{1,0:T(1,128)} %table_hbm.1, bf16[8,128]{1,0:T(8,128)(2,1)} %bitcast.22, f32[64,1,128]{2,1,0:T(1,128)} %kscale_hbm.1, s32[8,64]{1,0:T(8,128)} %bitcast.23, ...), custom_call_target="tpu_custom_call" | custom-call | flops 268435456 | bytes 10485760 | tf_op jit(solution)/shard_map/prepare/pallas_call | solution.py:373
  26.4 9.2 %all-to-all-done = bf16[64,8,128]{2,1,0:T(8,128)(2,1)S(1)} async-done(((bf16[64,8,128]{2,1,0:T(8,128)(2,1)}), bf16[64,8,128]{2,1,0:T(8,128)(2,1)S(1)}, u32[]{:S(2)}, u32[]{:S(2)}) %all-to-all-start) | async-done | bytes 131104 | tf_op jit(solution)/shard_map/all_to_all | solution.py:355
  35.5 0.0 copy-start
  35.5 7.0 %attend.1 = bf16[8,72,128]{2,1,0:T(8,128)(2,1)S(1)} custom-call(s32[1]{0:T(128)} %bitcast.place_ref, bf16[512,128]{1,0:T(8,128)(2,1)S(1)} %bitcast.14, f32[256,3,8,128]{3,2,1,0:T(8,128)} %get-tuple-element.8.own_hbm, bf16[8192,128]{1,0:T(8,128)(2,1)} %get-tuple-element.9.keys_hbm, bf16[8192,128]{1,0:T(8,128)(2,1)} %get-tuple-element.10.values_hbm), custom_call_target="tpu_custom_call" | custom-call | tf_op jit(solution)/shard_map/attend/pallas_call | solution.py:424
  42.6 9.2 %all_to_all.25.in_ref = bf16[8,72,128]{2,1,0:T(8,128)(2,1)S(1)} all-to-all(bf16[8,72,128]{2,1,0:T(8,128)(2,1)S(1)} %attend.1), channel_id=1, replica_groups=mesh['zh'=8,'zl'=2,'y'=4,'x'=4,'core'=2] {'zl','y'}, dimensions={0} | all-to-all | bytes 294912 | tf_op jit(solution)/shard_map/all_to_all | solution.py:479
  51.7 0.4 merge_near.1
  52.1 17.4 %all_to_all.26.in_ref = bf16[8,72,128]{2,1,0:T(8,128)(2,1)S(1)} all-to-all(bf16[8,72,128]{2,1,0:T(8,128)(2,1)S(1)} %merge_near.1), channel_id=1, replica_groups=mesh['zh'=8,'zl'=2,'y'=4,'x'=4,'core'=2] {'zh'}, dimensions={0} | all-to-all | bytes 294912 | tf_op jit(solution)/shard_map/all_to_all | solution.py:488
  69.5 0.3 merge_far.1
  69.8 7.8 %all_to_all.27.in_ref = bf16[8,64,128]{2,1,0:T(8,128)(2,1)S(1)} all-to-all(bf16[8,64,128]{2,1,0:T(8,128)(2,1)S(1)} %merge_far.1), channel_id=1, replica_groups=mesh['zh'=8,'zl'=2,'y'=4,'x'=4,'core'=2] {'zl','y'}, dimensions={0} | all-to-all | bytes 262144 | tf_op jit(solution)/shard_map/all_to_all | solution.py:497
  77.6 0.0 copy-done
  77.6 0.2 project.1
  77.8 13.8 %all_to_all.28.in_ref = bf16[8,8,128]{2,1,0:T(8,128)(2,1)S(1)} all-to-all(bf16[8,8,128]{2,1,0:T(8,128)(2,1)S(1)} %bitcast.15), channel_id=1, replica_groups=mesh['zh'=8,'zl'=2,'y'=4,'x'=4,'core'=2] {'x','core'}, dimensions={0} | all-to-all | bytes 32768 | tf_op jit(solution)/shard_map/all_to_all | solution.py:508
  91.7 0.6 sum_tp.1
Async XLA Ops:
  1.3 34.2 %all-to-all-start = ((bf16[64,8,128]{2,1,0:T(8,128)(2,1)}), bf16[64,8,128]{2,1,0:T(8,128)(2,1)S(1)}, u32[]{:S(2)}, u32[]{:S(2)}) async-start(bf16[64,8,128]{2,1,0:T(8,128)(2,1)} %broadcast_in_dim.8), calls=%async_computation | async-start | bytes 262144 | tf_op jit(solution)/shard_map/all_to_all | solution.py:355
  35.5 42.1 %copy-start = (bf16[1024,128]{1,0:T(8,128)(2,1)S(1)}, bf16[1024,128]{1,0:T(8,128)(2,1)}, u32[]{:S(2)}) copy-start(bf16[1024,128]{1,0:T(8,128)(2,1)} %weight_ref.1) | copy-start | bytes 786436

commit v9 on v8

--- a/solution.py
+++ b/solution.py
@@ -456,7 +456,7 @@
     suffix_len,
     out_weight,
 ):
-    seq, near, far = ("zh", "zl", "y"), ("zl", "y"), "zh"
+    seq, near, far = ("zt", "zs", "zm", "zl", "y"), ("zl", "y"), ("zm", "zs", "zt")
     samples = lax.axis_size(seq)
     queries = queries.reshape(HEADS, LANES)
     all_queries = spread(queries, seq).reshape(samples * HEADS, LANES)
@@ -517,8 +517,8 @@
 
 
 def solution(mesh):
-    grid = Mesh(mesh.devices.reshape(8, 2, 4, 4, 2), ("zh", "zl", "y", "x", "core"))
-    seq, tp = ("zh", "zl", "y"), ("x", "core")
+    grid = Mesh(mesh.devices.reshape(2, 2, 2, 2, 4, 4, 2), ("zt", "zs", "zm", "zl", "y", "x", "core"))
+    seq, tp = ("zt", "zs", "zm", "zl", "y"), ("x", "core")
     return jax.shard_map(
         shards,
         mesh=grid,

time: 92.6 us -> 90.8 us (0.981)
  blocking collectives: 48.2 us -> 46.5 us
    all_to_all x1, blocking collectives: 17.4 us -> 15.5 us  [shards(): partial = lax.all_to_all(partial, far, 0, 0)]
where the time goes in v9:
time: 90.8 us; the launch traced here: 90.5 us
  blocking collectives  46.5 us (51%)
  starting transfers between devices  19.3 us (21%)
  Pallas kernels  13.6 us (15%)
  waiting for transfers between devices  9.16 us (10%)
  local copies, waits for them, and re-layouts  1.35 us (1%)
    all_to_all x1, starting transfers between devices, spread(): return lax.all_to_all(copies, axis, 0, 0)  19.3 us
    all_to_all x1, blocking collectives, shards(): partial = lax.all_to_all(partial, far, 0, 0)  15.5 us
    all_to_all x1, blocking collectives, shards(): lax.all_to_all(product.reshape(tp, samples // tp, LANES), ('x', 'core'),...  13.5 us
    all_to_all x1, blocking collectives, shards(): partial = lax.all_to_all(partial, near, 0, 0)  9.16 us
    all_to_all x1, waiting for transfers between devices, spread(): return lax.all_to_all(copies, axis, 0, 0)  9.16 us
    all_to_all x1, blocking collectives, shards(): attention = lax.all_to_all(attention, near, 0, 0)  8.36 us
    pallas_call x1, Pallas kernels, attend(): pl.pallas_call(attend_kernel, out_shape=jax.ShapeDtypeStruct((rows // GRO...  7 us
    pallas_call x1, Pallas kernels, prepare(): pl.pallas_call(prepare_kernel, out_shape=(jax.ShapeDtypeStruct((keys, LAN...  5.08 us
  transfers between devices with their start and end apart: 1, of which 1 were waited for; matrix products, arithmetic and copies ran while one was open for 0% of the time, Pallas kernels for 6%

profile of v9, /device:TPU:1, one launch (start us, length us, event | category | flops | bytes accessed | tf_op | source)
XLA Modules:
  0.0 90.5 jit_solution(5133625898897690796)
XLA Ops:
  0.0 1.3 %broadcast_in_dim.8 = bf16[64,8,128]{2,1,0:T(8,128)(2,1)} broadcast(bf16[8,128]{1,0:T(8,128)(2,1)} %bitcast.21), dimensions={1,2} | broadcast | bytes 133120 | tf_op jit(solution)/shard_map/broadcast_in_dim | solution.py:354
  1.3 19.3 %all-to-all-start = ((bf16[64,8,128]{2,1,0:T(8,128)(2,1)}), bf16[64,8,128]{2,1,0:T(8,128)(2,1)S(1)}, u32[]{:S(2)}, u32[]{:S(2)}) async-start(bf16[64,8,128]{2,1,0:T(8,128)(2,1)} %broadcast_in_dim.8), calls=%async_computation | async-start | bytes 262144 | tf_op jit(solution)/shard_map/all_to_all | solution.py:355
  21.3 5.1 %prepare.1 = (bf16[8192,128]{1,0:T(8,128)(2,1)}, bf16[8192,128]{1,0:T(8,128)(2,1)}, f32[256,3,8,128]{3,2,1,0:T(8,128)}) custom-call(s32[1]{0:T(128)S(6)} %copy.13.len_hbm, s32[1,4]{1,0:T(1,128)} %table_hbm.1, bf16[8,128]{1,0:T(8,128)(2,1)} %bitcast.22, f32[64,1,128]{2,1,0:T(1,128)} %kscale_hbm.1, s32[8,64]{1,0:T(8,128)} %bitcast.23, ...), custom_call_target="tpu_custom_call" | custom-call | flops 268435456 | bytes 10485760 | tf_op jit(solution)/shard_map/prepare/pallas_call | solution.py:373
  26.4 9.2 %all-to-all-done = bf16[64,8,128]{2,1,0:T(8,128)(2,1)S(1)} async-done(((bf16[64,8,128]{2,1,0:T(8,128)(2,1)}), bf16[64,8,128]{2,1,0:T(8,128)(2,1)S(1)}, u32[]{:S(2)}, u32[]{:S(2)}) %all-to-all-start) | async-done | bytes 131104 | tf_op jit(solution)/shard_map/all_to_all | solution.py:355
  35.5 0.0 copy-start
  35.5 7.0 %attend.1 = bf16[8,72,128]{2,1,0:T(8,128)(2,1)S(1)} custom-call(s32[1]{0:T(128)} %bitcast.place_ref, bf16[512,128]{1,0:T(8,128)(2,1)S(1)} %bitcast.14, f32[256,3,8,128]{3,2,1,0:T(8,128)} %get-tuple-element.8.own_hbm, bf16[8192,128]{1,0:T(8,128)(2,1)} %get-tuple-element.9.keys_hbm, bf16[8192,128]{1,0:T(8,128)(2,1)} %get-tuple-element.10.values_hbm), custom_call_target="tpu_custom_call" | custom-call | tf_op jit(solution)/shard_map/attend/pallas_call | solution.py:424
  42.6 9.2 %all_to_all.25.in_ref = bf16[8,72,128]{2,1,0:T(8,128)(2,1)S(1)} all-to-all(bf16[8,72,128]{2,1,0:T(8,128)(2,1)S(1)} %attend.1), channel_id=1, replica_groups=mesh['zt'=2,'zs'=2,'zm'=2,'zl'=2,'y'=4,'x'=4,'core'=2] {'zl','y'}, dimensions={0} | all-to-all | bytes 294912 | tf_op jit(solution)/shard_map/all_to_all | solution.py:479
  51.7 0.4 merge_near.1
  52.1 15.5 %all_to_all.26.in_ref = bf16[8,72,128]{2,1,0:T(8,128)(2,1)S(1)} all-to-all(bf16[8,72,128]{2,1,0:T(8,128)(2,1)S(1)} %merge_near.1), channel_id=1, replica_groups=mesh['zt'=2,'zs'=2,'zm'=2,'zl'=2,'y'=4,'x'=4,'core'=2] {'zm','zs','zt'}, dimensions={0} | all-to-all | bytes 294912 | tf_op jit(solution)/shard_map/all_to_all | solution.py:488
  67.5 0.3 merge_far.1
  67.9 8.4 %all_to_all.27.in_ref = bf16[8,64,128]{2,1,0:T(8,128)(2,1)S(1)} all-to-all(bf16[8,64,128]{2,1,0:T(8,128)(2,1)S(1)} %merge_far.1), channel_id=1, replica_groups=mesh['zt'=2,'zs'=2,'zm'=2,'zl'=2,'y'=4,'x'=4,'core'=2] {'zl','y'}, dimensions={0} | all-to-all | bytes 262144 | tf_op jit(solution)/shard_map/all_to_all | solution.py:497
  76.2 0.0 copy-done
  76.2 0.2 project.1
  76.4 13.5 %all_to_all.28.in_ref = bf16[8,8,128]{2,1,0:T(8,128)(2,1)S(1)} all-to-all(bf16[8,8,128]{2,1,0:T(8,128)(2,1)S(1)} %bitcast.15), channel_id=1, replica_groups=mesh['zt'=2,'zs'=2,'zm'=2,'zl'=2,'y'=4,'x'=4,'core'=2] {'x','core'}, dimensions={0} | all-to-all | bytes 32768 | tf_op jit(solution)/shard_map/all_to_all | solution.py:508
  89.9 0.6 sum_tp.1
Async XLA Ops:
  1.3 34.2 %all-to-all-start = ((bf16[64,8,128]{2,1,0:T(8,128)(2,1)}), bf16[64,8,128]{2,1,0:T(8,128)(2,1)S(1)}, u32[]{:S(2)}, u32[]{:S(2)}) async-start(bf16[64,8,128]{2,1,0:T(8,128)(2,1)} %broadcast_in_dim.8), calls=%async_computation | async-start | bytes 262144 | tf_op jit(solution)/shard_map/all_to_all | solution.py:355
  35.5 40.7 %copy-start = (bf16[1024,128]{1,0:T(8,128)(2,1)S(1)}, bf16[1024,128]{1,0:T(8,128)(2,1)}, u32[]{:S(2)}) copy-start(bf16[1024,128]{1,0:T(8,128)(2,1)} %weight_ref.1) | copy-start | bytes 786436

commit v10 on v9

--- a/solution.py
+++ b/solution.py
@@ -16,6 +16,7 @@
 TILE = 256
 BLOCK = 2048
 WEIGHT_STEP = 1024
+WIDTH = 4
 ROOM = 256
 PAGES = BLOCK // PAGE
 SCORE_SCALE = math.log2(math.e) / math.sqrt(LANES)
@@ -65,6 +66,12 @@
     row = lax.broadcasted_iota(jnp.int32, wide.shape, 0)
     lane = lax.broadcasted_iota(jnp.int32, wide.shape, 1)
     return jnp.sum(jnp.where(lane % SPLIT == row, wide, 0.0), axis=1, keepdims=True)
+
+
+def place_of(c, u, pieces, depth):
+    low, y = c // WIDTH, c % WIDTH
+    pairs = pieces // WIDTH
+    return (y * depth + u) * pairs + low
 
 
 def prepare_kernel(
@@ -293,8 +300,8 @@
     pieces = out_ref.shape[0]
     for c in range(pieces):
         rows = [
-            slice((u * pieces + c) * HEADS, (u * pieces + c + 1) * HEADS)
-            for u in range(GROUP // HEADS)
+            slice(at * HEADS, (at + 1) * HEADS)
+            for at in (place_of(c, u, pieces, GROUP // HEADS) for u in range(GROUP // HEADS))
         ]
         part = [acc[r, :] / total[r, :] for r in rows]
         logs = [peak[r, :] + jnp.log2(total[r, :]) for r in rows]
@@ -457,10 +464,11 @@
     out_weight,
 ):
     seq, near, far = ("zt", "zs", "zm", "zl", "y"), ("zl", "y"), ("zm", "zs", "zt")
+    gather = ("y", "zt", "zs", "zm", "zl")
     samples = lax.axis_size(seq)
     queries = queries.reshape(HEADS, LANES)
-    all_queries = spread(queries, seq).reshape(samples * HEADS, LANES)
-    own = lax.axis_index(seq).astype(jnp.int32).reshape(1)
+    all_queries = spread(queries, gather).reshape(samples * HEADS, LANES)
+    own = lax.axis_index(gather).astype(jnp.int32).reshape(1)
     params = pltpu.CompilerParams(vmem_limit_bytes=SMALL)
     prepared = prepare(
         queries,

time: 90.8 us -> 90.8 us (level)
  waiting for transfers between devices: 9.16 us -> 8.22 us
    all_to_all x1, blocking collectives: 9.16 us -> 10.6 us  [shards(): partial = lax.all_to_all(partial, near, 0, 0)]
    all_to_all x1, waiting for transfers between devices: 9.16 us -> 8.22 us  [spread(): return lax.all_to_all(copies, axis, 0, 0)]
where the time goes in v10:
time: 90.8 us; the launch traced here: 90.4 us
  blocking collectives  47.3 us (52%)
  starting transfers between devices  19.3 us (21%)
  Pallas kernels  13.6 us (15%)
  waiting for transfers between devices  8.22 us (9%)
  local copies, waits for them, and re-layouts  1.35 us (1%)
    all_to_all x1, starting transfers between devices, spread(): return lax.all_to_all(copies, axis, 0, 0)  19.3 us
    all_to_all x1, blocking collectives, shards(): partial = lax.all_to_all(partial, far, 0, 0)  14.8 us
    all_to_all x1, blocking collectives, shards(): lax.all_to_all(product.reshape(tp, samples // tp, LANES), ('x', 'core'),...  13.5 us
    all_to_all x1, blocking collectives, shards(): partial = lax.all_to_all(partial, near, 0, 0)  10.6 us
    all_to_all x1, blocking collectives, shards(): attention = lax.all_to_all(attention, near, 0, 0)  8.46 us
    all_to_all x1, waiting for transfers between devices, spread(): return lax.all_to_all(copies, axis, 0, 0)  8.22 us
    pallas_call x1, Pallas kernels, attend(): pl.pallas_call(attend_kernel, out_shape=jax.ShapeDtypeStruct((rows // GRO...  7 us
    pallas_call x1, Pallas kernels, prepare(): pl.pallas_call(prepare_kernel, out_shape=(jax.ShapeDtypeStruct((keys, LAN...  5.08 us
  transfers between devices with their start and end apart: 1, of which 1 were waited for; matrix products, arithmetic and copies ran while one was open for 0% of the time, Pallas kernels for 6%

profile of v10, /device:TPU:1, one launch (start us, length us, event | category | flops | bytes accessed | tf_op | source)
XLA Modules:
  0.0 90.4 jit_solution(2422053516311769942)
XLA Ops:
  0.0 1.3 %broadcast_in_dim.8 = bf16[64,8,128]{2,1,0:T(8,128)(2,1)} broadcast(bf16[8,128]{1,0:T(8,128)(2,1)} %bitcast.21), dimensions={1,2} | broadcast | bytes 133120 | tf_op jit(solution)/shard_map/broadcast_in_dim | solution.py:361
  1.3 19.3 %all-to-all-start = ((bf16[64,8,128]{2,1,0:T(8,128)(2,1)}), bf16[64,8,128]{2,1,0:T(8,128)(2,1)S(1)}, u32[]{:S(2)}, u32[]{:S(2)}) async-start(bf16[64,8,128]{2,1,0:T(8,128)(2,1)} %broadcast_in_dim.8), calls=%async_computation | async-start | bytes 262144 | tf_op jit(solution)/shard_map/all_to_all | solution.py:362
  21.3 5.1 %prepare.1 = (bf16[8192,128]{1,0:T(8,128)(2,1)}, bf16[8192,128]{1,0:T(8,128)(2,1)}, f32[256,3,8,128]{3,2,1,0:T(8,128)}) custom-call(s32[1]{0:T(128)S(6)} %copy.13.len_hbm, s32[1,4]{1,0:T(1,128)} %table_hbm.1, bf16[8,128]{1,0:T(8,128)(2,1)} %bitcast.22, f32[64,1,128]{2,1,0:T(1,128)} %kscale_hbm.1, s32[8,64]{1,0:T(8,128)} %bitcast.23, ...), custom_call_target="tpu_custom_call" | custom-call | flops 268435456 | bytes 10485760 | tf_op jit(solution)/shard_map/prepare/pallas_call | solution.py:380
  26.4 8.2 %all-to-all-done = bf16[64,8,128]{2,1,0:T(8,128)(2,1)S(1)} async-done(((bf16[64,8,128]{2,1,0:T(8,128)(2,1)}), bf16[64,8,128]{2,1,0:T(8,128)(2,1)S(1)}, u32[]{:S(2)}, u32[]{:S(2)}) %all-to-all-start) | async-done | bytes 131104 | tf_op jit(solution)/shard_map/all_to_all | solution.py:362
  34.6 0.0 copy-start
  34.6 7.0 %attend.1 = bf16[8,72,128]{2,1,0:T(8,128)(2,1)S(1)} custom-call(s32[1]{0:T(128)} %bitcast.place_ref, bf16[512,128]{1,0:T(8,128)(2,1)S(1)} %bitcast.14, f32[256,3,8,128]{3,2,1,0:T(8,128)} %get-tuple-element.8.own_hbm, bf16[8192,128]{1,0:T(8,128)(2,1)} %get-tuple-element.9.keys_hbm, bf16[8192,128]{1,0:T(8,128)(2,1)} %get-tuple-element.10.values_hbm), custom_call_target="tpu_custom_call" | custom-call | tf_op jit(solution)/shard_map/attend/pallas_call | solution.py:431
  41.6 10.6 %all_to_all.25.in_ref = bf16[8,72,128]{2,1,0:T(8,128)(2,1)S(1)} all-to-all(bf16[8,72,128]{2,1,0:T(8,128)(2,1)S(1)} %attend.1), channel_id=1, replica_groups=mesh['zt'=2,'zs'=2,'zm'=2,'zl'=2,'y'=4,'x'=4,'core'=2] {'zl','y'}, dimensions={0} | all-to-all | bytes 294912 | tf_op jit(solution)/shard_map/all_to_all | solution.py:487
  52.2 0.4 merge_near.1
  52.5 14.8 %all_to_all.26.in_ref = bf16[8,72,128]{2,1,0:T(8,128)(2,1)S(1)} all-to-all(bf16[8,72,128]{2,1,0:T(8,128)(2,1)S(1)} %merge_near.1), channel_id=1, replica_groups=mesh['zt'=2,'zs'=2,'zm'=2,'zl'=2,'y'=4,'x'=4,'core'=2] {'zm','zs','zt'}, dimensions={0} | all-to-all | bytes 294912 | tf_op jit(solution)/shard_map/all_to_all | solution.py:496
  67.3 0.3 merge_far.1
  67.7 8.5 %all_to_all.27.in_ref = bf16[8,64,128]{2,1,0:T(8,128)(2,1)S(1)} all-to-all(bf16[8,64,128]{2,1,0:T(8,128)(2,1)S(1)} %merge_far.1), channel_id=1, replica_groups=mesh['zt'=2,'zs'=2,'zm'=2,'zl'=2,'y'=4,'x'=4,'core'=2] {'zl','y'}, dimensions={0} | all-to-all | bytes 262144 | tf_op jit(solution)/shard_map/all_to_all | solution.py:505
  76.1 0.0 copy-done
  76.1 0.2 project.1
  76.3 13.5 %all_to_all.28.in_ref = bf16[8,8,128]{2,1,0:T(8,128)(2,1)S(1)} all-to-all(bf16[8,8,128]{2,1,0:T(8,128)(2,1)S(1)} %bitcast.15), channel_id=1, replica_groups=mesh['zt'=2,'zs'=2,'zm'=2,'zl'=2,'y'=4,'x'=4,'core'=2] {'x','core'}, dimensions={0} | all-to-all | bytes 32768 | tf_op jit(solution)/shard_map/all_to_all | solution.py:516
  89.8 0.6 sum_tp.1
Async XLA Ops:
  1.3 33.3 %all-to-all-start = ((bf16[64,8,128]{2,1,0:T(8,128)(2,1)}), bf16[64,8,128]{2,1,0:T(8,128)(2,1)S(1)}, u32[]{:S(2)}, u32[]{:S(2)}) async-start(bf16[64,8,128]{2,1,0:T(8,128)(2,1)} %broadcast_in_dim.8), calls=%async_computation | async-start | bytes 262144 | tf_op jit(solution)/shard_map/all_to_all | solution.py:362
  34.6 41.5 %copy-start = (bf16[1024,128]{1,0:T(8,128)(2,1)S(1)}, bf16[1024,128]{1,0:T(8,128)(2,1)}, u32[]{:S(2)}) copy-start(bf16[1024,128]{1,0:T(8,128)(2,1)} %weight_ref.1) | copy-start | bytes 786436
